TPU v7x, 256 devices: a whole 4x4x8 slice. The times are simulated.
256 devices in a mesh: group: 16 (over z, core), tensor: 4 (over x), seq: 4 (over y).
Axes of the slice: x: 4, y: 4, z: 8, core: 2. Of those that a mesh axis runs over, the one named last changes fastest.
Arguments:
- hidden: bfloat16 [4096, 8192], P('group', ('tensor', 'seq')), may hold values from -6 to 6
- key_value_weight: bfloat16 [8192, 8, 2, 128], P(('tensor', 'seq')), may hold values from -0.0625 to 0.0625
- adapter_down_weight: bfloat16 [64, 8192, 128], P('group', ('tensor', 'seq')), may hold values from -0.0625 to 0.0625
- adapter_up_weight: bfloat16 [64, 2, 64, 1024], P('group', None, None, 'tensor'), may hold values from -0.75 to 0.75
- queries: bfloat16 [4096, 8192], P('group', 'tensor'), may hold values from -120 to 120
- key_value_cache: bfloat16 [32, 16384, 8, 2, 128], P('group', 'seq', 'tensor'), may hold values from -6.08 to 6.08
- request_adapter: int32 [32], replicated, may hold values from 0 to 63
Outputs:
- new_kv: bfloat16 [4096, 8, 2, 128], P(('group', 'seq'), 'tensor')
- attention: bfloat16 [4096, 8192], P(('group', 'seq'), 'tensor')
All inputs are finite; a program needn't handle non-finite values.
Results may differ from a plain program's by a relative error of at most 0.012.
Values may be sent and summed in bfloat16 or wider, within the bound.
No kernel may reach another device: no remote copies, remote signals or barrier semaphores. Data moves between devices by JAX's collectives and lax.ppermute only.
A program may use at most 192 MiB of HBM per device.

v0:
```python
import functools
import math

import jax
import jax.numpy as jnp
from jax import lax
from jax.experimental import pallas as pl
from jax.experimental.pallas import tpu as pltpu
from jax.sharding import PartitionSpec as P

NEW_TOK = 128
CACHE = 16384
WIDTH = 128
SCALE = math.log2(math.e) / math.sqrt(WIDTH)
KEY_BLOCK = 4096
BODY = 4
TILE = 256
LOW = -1e30
BF = jnp.bfloat16
F32 = jnp.float32
ATTEND_VMEM = 44 * 2**20
SMALL_VMEM = 16 * 2**20

SEQ, HALF, PARITY, TENSOR, PLANE, CORE, ADAPTERS = 0, 1, 2, 3, 4, 5, 6


def prep_kernel(where, hidden_far, weight_far, cache_far, query_far, *rest):
    outs, (cache_out, query_out, hidden_ref, weight_ref, cols, sem) = rest[:4], rest[4:]
    loads = [
        pltpu.make_async_copy(far, near, sem.at[n])
        for n, (far, near) in enumerate(
            (
                (weight_far, weight_ref),
                (hidden_far, hidden_ref),
                (query_far, query_out),
                (cache_far, cache_out),
            )
        )
    ]
    for load in loads:
        load.start()
    for load in loads[:2]:
        load.wait()
    depth = hidden_ref.shape[1]
    rows = weight_ref[...].astype(F32).reshape(depth // 8, 8, 2, 8, WIDTH)
    place = lax.broadcasted_iota(jnp.int32, (depth // 8, 8, WIDTH), 1)
    for a in range(2):
        parts = [rows[:, j, a] for j in range(8)]
        for bit in (1, 2, 4):
            odd = (place & bit) != 0
            for j in range(8):
                if not j & bit:
                    low, high = parts[j], parts[j | bit]
                    parts[j] = jnp.where(odd, pltpu.roll(high, bit, 1), low)
                    parts[j | bit] = jnp.where(odd, high, pltpu.roll(low, 8 - bit, 1))
        for c in range(8):
            dest, part = 2 * a + c // 4, c % 4
            cols[dest, :, part * WIDTH : (part + 1) * WIDTH] = (
                parts[c].reshape(depth, WIDTH).astype(BF)
            )
    for step in range(4):
        dest = lax.rem(where[TENSOR] + step, 4)
        outs[step][...] = jnp.dot(
            hidden_ref[...], cols[dest], preferred_element_type=F32
        ).astype(BF)
    for load in loads[2:]:
        load.wait()


def in_hbm(a):
    return pltpu.with_memory_space_constraint(a, pltpu.HBM)


def prep(where, hidden, weight_rows, cache_rows, queries):
    tokens, depth = hidden.shape
    whole = pl.BlockSpec(memory_space=pltpu.VMEM)
    anywhere = pl.BlockSpec(memory_space=pl.ANY)
    return pl.pallas_call(
        prep_kernel,
        in_specs=[pl.BlockSpec(memory_space=pltpu.SMEM)] + [anywhere] * 4,
        out_specs=[whole] * 6,
        out_shape=[jax.ShapeDtypeStruct((tokens, 4 * WIDTH), BF)] * 4
        + [pltpu.VMEM(cache_rows.shape, BF), pltpu.VMEM(queries.shape, BF)],
        scratch_shapes=[
            pltpu.VMEM(hidden.shape, BF),
            pltpu.VMEM(weight_rows.shape, BF),
            pltpu.VMEM((4, depth, 4 * WIDTH), BF),
            pltpu.SemaphoreType.DMA((4,)),
        ],
        compiler_params=pltpu.CompilerParams(vmem_limit_bytes=SMALL_VMEM),
        cost_estimate=pl.CostEstimate(
            flops=2 * tokens * depth * 16 * WIDTH, bytes_accessed=11 * 2**20, transcendentals=0
        ),
        name="base_partial",
    )(where, *map(in_hbm, (hidden, weight_rows, cache_rows, queries)))


def attend_kernel(where, q_ref, x_ref, o_first, o_second, acc, top, wide, keys, values):
    block = pl.program_id(0)
    tokens = q_ref.shape[0]
    per_tile = TILE // tokens
    tiles = 8 // per_tile

    @pl.when(block == 0)
    def _():
        acc[...] = jnp.zeros_like(acc)
        top[...] = jnp.full_like(top, LOW)
        for h in range(2):
            values[h, :, WIDTH:] = jnp.ones((KEY_BLOCK, WIDTH), BF)

    wide[...] = x_ref[...].astype(F32)
    for h in range(2):
        keys[h] = wide[pl.ds(2 * h, KEY_BLOCK, stride=4), :].astype(BF)
        values[h, :, :WIDTH] = wide[pl.ds(2 * h + 1, KEY_BLOCK, stride=4), :].astype(BF)

    def score(h, t):
        first = h * 8 + t * per_tile
        q = jnp.concatenate(
            [
                q_ref[:, pl.ds(pl.multiple_of((first + j) * WIDTH, WIDTH), WIDTH)]
                for j in range(per_tile)
            ],
            axis=0,
        )
        return lax.dot_general(q, keys[h], (((1,), (1,)), ((), ())), preferred_element_type=F32)

    def absorb(h, t, s):
        i = h * tiles + t
        before = top[i]
        after = jnp.maximum(before, jnp.max(s, axis=1, keepdims=True) * SCALE)
        top[i] = after
        fade = jnp.exp2(before - after)
        p = jnp.exp2(s * SCALE - after[:, :1]).astype(BF)
        acc[i] = acc[i] * jnp.concatenate([fade, fade], axis=1) + jnp.dot(
            p, values[h], preferred_element_type=F32
        )

    def turn(k, _):
        h, start = k // (tiles // BODY), k % (tiles // BODY) * BODY
        ahead = []
        for t in range(0, BODY, 2):
            now = [(start + u, score(h, start + u)) for u in (t, t + 1)]
            for job in ahead:
                absorb(h, *job)
            ahead = now
        for job in ahead:
            absorb(h, *job)
        return 0

    lax.fori_loop(0, 2 * tiles // BODY, turn, 0)

    @pl.when(block == pl.num_programs(0) - 1)
    def _():
        half = tokens // 2
        odd = where[PARITY] == 1
        lane = lax.broadcasted_iota(jnp.int32, (tokens, WIDTH), 1)
        logs = jnp.zeros((tokens, WIDTH), F32)
        for h in range(2):
            for t in range(tiles):
                i = h * tiles + t
                total = acc[i, :, WIDTH:]
                mean = (acc[i, :, :WIDTH] / total).astype(BF)
                log = top[i] + jnp.log2(total)
                for j in range(per_tile):
                    n = h * 8 + t * per_tile + j
                    early = mean[j * tokens : j * tokens + half]
                    late = mean[j * tokens + half : (j + 1) * tokens]
                    cols = slice(n * WIDTH, (n + 1) * WIDTH)
                    o_first[:, cols] = jnp.where(odd, late, early)
                    o_second[:, cols] = jnp.where(odd, early, late)
                    logs = jnp.where(lane == n, log[j * tokens : (j + 1) * tokens], logs)
        high = logs.astype(BF).astype(F32)
        middle = (logs - high).astype(BF).astype(F32)
        low = logs - high - middle
        logs = (high + pltpu.roll(middle, 16, 1) + pltpu.roll(low, 32, 1)).astype(BF)
        o_first[:, 16 * WIDTH :] = jnp.where(odd, logs[half:], logs[:half])
        o_second[:, 16 * WIDTH :] = jnp.where(odd, logs[:half], logs[half:])


def attend(where, queries, cache_rows, other):
    tokens, width = NEW_TOK, queries.shape[1]
    blocks = cache_rows.shape[0] // 2 // 4 // KEY_BLOCK
    tiles = 16 * tokens // TILE

    def request(w):
        return 1 - w[HALF] if other else w[HALF]

    o = jax.ShapeDtypeStruct((tokens // 2, width + WIDTH), BF)
    scores = 16 * tokens * blocks * KEY_BLOCK
    return pl.pallas_call(
        attend_kernel,
        grid_spec=pltpu.PrefetchScalarGridSpec(
            num_scalar_prefetch=1,
            grid=(blocks,),
            in_specs=[
                pl.BlockSpec((tokens, width), lambda i, w: (request(w), 0)),
                pl.BlockSpec((KEY_BLOCK * 4, WIDTH), lambda i, w: (request(w) * blocks + i, 0)),
            ],
            out_specs=[pl.BlockSpec(o.shape, lambda i, w: (0, 0))] * 2,
            scratch_shapes=[
                pltpu.VMEM((tiles, TILE, 2 * WIDTH), F32),
                pltpu.VMEM((tiles, TILE, WIDTH), F32),
                pltpu.VMEM((KEY_BLOCK * 4, WIDTH), F32),
                pltpu.VMEM((2, KEY_BLOCK, WIDTH), BF),
                pltpu.VMEM((2, KEY_BLOCK, 2 * WIDTH), BF),
            ],
        ),
        out_shape=[o, o],
        compiler_params=pltpu.CompilerParams(vmem_limit_bytes=ATTEND_VMEM),
        cost_estimate=pl.CostEstimate(
            flops=scores * WIDTH * 8, bytes_accessed=5 * 2**20, transcendentals=scores
        ),
        name="attend_other" if other else "attend_own",
    )(where, queries, cache_rows)


def owner(where, plane, r):
    return where[ADAPTERS + 2 * (2 * plane + where[CORE]) + r]


def when_mine(where, adapter, maps, out, sem):
    down, up, mate_down, mate_up = maps
    mine = adapter // 8 == where[PLANE]
    mates = adapter // 4 % 2 != where[CORE]
    k = adapter % 4
    depth = down.shape[1]
    cols = pl.ds(pl.multiple_of(where[PARITY] * WIDTH, WIDTH), WIDTH)

    def pair(downs, ups):
        return (
            pltpu.make_async_copy(downs.at[k], out.at[:depth], sem.at[0]),
            pltpu.make_async_copy(ups.at[k, where[HALF], :, cols], out.at[depth:], sem.at[1]),
        )

    def start():
        @pl.when(jnp.logical_and(mine, mates))
        def _():
            for copy in pair(mate_down, mate_up):
                copy.start()

        @pl.when(jnp.logical_and(mine, jnp.logical_not(mates)))
        def _():
            for copy in pair(down, up):
                copy.start()

    def wait():
        @pl.when(mine)
        def _():
            for copy in pair(down, up):
                copy.wait()

    return mine, start, wait


def relay_kernel(slots, arrivals, where, *refs):
    maps, came, outs, sem = refs[:4], refs[4 : 4 + arrivals], refs[4 + arrivals : -1], refs[-1]
    waits = []
    for n, (way, slot, hops, r, arrival) in enumerate(slots):
        plane = lax.rem(where[PLANE] + hops + 8, 8)
        out = outs[way].at[slot]
        mine, start, wait = when_mine(where, owner(where, plane, r), maps, out, sem.at[n])
        start()
        waits.append(wait)
        if arrival is not None:

            @pl.when(jnp.logical_not(mine))
            def _(out=out, arrival=arrival):
                out[...] = came[arrival[0]][arrival[1]]

    for wait in waits:
        wait()


def relay(where, maps, came, slots, name):
    height = maps[0].shape[1] + maps[1].shape[2]
    ways = 1 + max(slot[0] for slot in slots)
    outs = [
        jax.ShapeDtypeStruct((sum(slot[0] == way for slot in slots), height, WIDTH), BF)
        for way in range(ways)
    ]
    anywhere = pl.BlockSpec(memory_space=pl.ANY)
    whole = pl.BlockSpec(memory_space=pltpu.VMEM)
    return pl.pallas_call(
        functools.partial(relay_kernel, slots, len(came)),
        in_specs=[pl.BlockSpec(memory_space=pltpu.SMEM)] + [anywhere] * 4 + [whole] * len(came),
        out_specs=[whole] * ways,
        out_shape=outs,
        scratch_shapes=[pltpu.SemaphoreType.DMA((len(slots), 2))],
        compiler_params=pltpu.CompilerParams(vmem_limit_bytes=SMALL_VMEM),
        cost_estimate=pl.CostEstimate(
            flops=0, bytes_accessed=2 * 2**20, transcendentals=0
        ),
        name=name,
    )(where, *map(in_hbm, maps[:2]), *maps[2:], *came)


def rank_kernel(where, hidden_ref, base_ref, *refs):
    maps, came, (mine_out, others_out, held, sem) = refs[:4], refs[4:8], refs[8:]
    depth = hidden_ref.shape[1]
    height = held.shape[1] - depth
    waits = []
    for r in range(2):
        adapter = owner(where, where[PLANE], r)
        _, start, wait = when_mine(where, adapter, maps, held.at[r], sem.at[r])
        start()
        waits.append(wait)
        away = lax.rem(where[PLANE] + 8 - adapter // 8, 8)
        odd = away % 2 == 1
        below = away <= 4 if r == 0 else away < 4
        above = jnp.logical_not(below)
        even = jnp.logical_and(away != 0, jnp.logical_not(odd))
        for source, chosen in zip(
            came,
            (
                jnp.logical_and(odd, below),
                jnp.logical_and(even, below),
                jnp.logical_and(odd, above),
                jnp.logical_and(even, above),
            ),
        ):

            @pl.when(chosen)
            def _(r=r, source=source):
                held[r] = source[r]

    half = where[HALF]
    for out, request in ((mine_out, half), (others_out, 1 - half)):
        rows = pl.ds(pl.multiple_of(request * NEW_TOK, NEW_TOK), NEW_TOK)
        for part in range(4):
            start = NEW_TOK + height + part * NEW_TOK
            out[start : start + NEW_TOK] = base_ref[rows, part * WIDTH : (part + 1) * WIDTH]
    for wait in waits:
        wait()
    for out, request in ((mine_out, half), (others_out, 1 - half)):
        rows = pl.ds(pl.multiple_of(request * NEW_TOK, NEW_TOK), NEW_TOK)
        out[:NEW_TOK] = jnp.dot(
            hidden_ref[rows], held[request, :depth], preferred_element_type=F32
        ).astype(BF)
        out[NEW_TOK : NEW_TOK + height] = held[request, depth:]


def rank_parts(where, hidden, base, maps, came):
    height = came[0].shape[1]
    out = jax.ShapeDtypeStruct((5 * NEW_TOK + height - hidden.shape[1], WIDTH), BF)
    anywhere = pl.BlockSpec(memory_space=pl.ANY)
    whole = pl.BlockSpec(memory_space=pltpu.VMEM)
    return pl.pallas_call(
        rank_kernel,
        in_specs=[pl.BlockSpec(memory_space=pltpu.SMEM), whole, whole]
        + [anywhere] * 4
        + [whole] * 4,
        out_specs=[whole, whole],
        out_shape=[out, out],
        scratch_shapes=[pltpu.VMEM((2, height, WIDTH), BF), pltpu.SemaphoreType.DMA((2, 2))],
        compiler_params=pltpu.CompilerParams(vmem_limit_bytes=SMALL_VMEM),
        name="rank_partial",
    )(where, hidden, base, *map(in_hbm, maps[:2]), *maps[2:], *came)


def seq_kernel(where, *refs):
    parts, (rank_out, base_out, up_out) = refs[:4], refs[4:]
    after = NEW_TOK + up_out.shape[1]
    rank_out[...] = sum(part[:NEW_TOK].astype(F32) for part in parts).astype(BF)
    for step, part in enumerate(parts):
        up_out[jnp.bitwise_xor(where[SEQ], step)] = part[NEW_TOK:after]
    for col in range(4):
        start = after + col * NEW_TOK
        base_out[:, col * WIDTH : (col + 1) * WIDTH] = sum(
            part[start : start + NEW_TOK].astype(F32) for part in parts
        )


def seq_sum(where, parts):
    whole = pl.BlockSpec(memory_space=pltpu.VMEM)
    return pl.pallas_call(
        seq_kernel,
        in_specs=[pl.BlockSpec(memory_space=pltpu.SMEM)] + [whole] * 4,
        out_specs=[whole] * 3,
        out_shape=[
            jax.ShapeDtypeStruct((NEW_TOK, WIDTH), BF),
            jax.ShapeDtypeStruct((NEW_TOK, 4 * WIDTH), F32),
            jax.ShapeDtypeStruct((4, parts[0].shape[0] - 5 * NEW_TOK, WIDTH), BF),
        ],
        compiler_params=pltpu.CompilerParams(vmem_limit_bytes=SMALL_VMEM),
        name="seq_sum",
    )(where, *parts)


def merge_kernel(*refs):
    parts, mean_out, log_out = refs[:4], refs[4], refs[5]
    half = parts[0].shape[0]
    tops = []
    for part in parts:
        packed = part[:, 16 * WIDTH :].astype(F32)
        tops.append(packed + pltpu.roll(packed, WIDTH - 16, 1) + pltpu.roll(packed, WIDTH - 32, 1))
    top = functools.reduce(jnp.maximum, tops)
    weights = [jnp.exp2(l - top) for l in tops]
    total = sum(weights)
    merged = top + jnp.log2(total)
    weights = [w / total for w in weights]
    for n in range(16):
        rows = slice(n * half, (n + 1) * half)
        cols = slice(n * WIDTH, (n + 1) * WIDTH)
        mean_out[rows] = sum(
            w[:, n : n + 1] * part[:, cols].astype(F32) for w, part in zip(weights, parts)
        )
        log_out[rows] = jnp.broadcast_to(merged[:, n : n + 1], (half, WIDTH))


def merge(parts):
    out = jax.ShapeDtypeStruct((16 * parts[0].shape[0], WIDTH), F32)
    whole = pl.BlockSpec(memory_space=pltpu.VMEM)
    return pl.pallas_call(
        merge_kernel,
        in_specs=[whole] * 4,
        out_specs=[whole, whole],
        out_shape=[out, out],
        compiler_params=pltpu.CompilerParams(vmem_limit_bytes=SMALL_VMEM),
        name="merge_prefix",
    )(*parts)


def final_kernel(where, q_ref, cos_ref, sin_ref, up_ref, mean_ref, log_ref, base_ref, *rest):
    ranks, (kv_out, attention_out, wide) = rest[:4], rest[4:]
    half = q_ref.shape[0]
    start = pl.multiple_of(where[PARITY] * half, half)
    rank = sum(r[...].astype(F32) for r in ranks).astype(BF)
    keys, values = [], []
    for h in range(2):
        for e in range(2):
            delta = jnp.dot(
                rank[:, e * 64 : (e + 1) * 64], up_ref[2 * e + h], preferred_element_type=F32
            )
            part = 2 * h + e
            field = base_ref[:, part * WIDTH : (part + 1) * WIDTH] + delta
            if e == 0:
                field = field * cos_ref[...] + pltpu.roll(field, WIDTH // 2, 1) * sin_ref[...]
            wide[pl.ds(part, NEW_TOK, stride=4), :] = field
            (keys, values)[e].append(field.astype(BF))
    kv_out[...] = wide[pl.ds(start * 4, half * 4), :].astype(BF)
    rows = 8 * half
    token = lax.broadcasted_iota(jnp.int32, (rows, NEW_TOK), 0) % half + start
    seen = lax.broadcasted_iota(jnp.int32, (rows, NEW_TOK), 1) <= token
    ones = jnp.ones((NEW_TOK, WIDTH), BF)
    for h in range(2):
        q = jnp.concatenate(
            [q_ref[:, n * WIDTH : (n + 1) * WIDTH] for n in range(h * 8, h * 8 + 8)], axis=0
        )
        s = lax.dot_general(q, keys[h], (((1,), (1,)), ((), ())), preferred_element_type=F32)
        s = jnp.where(seen, s * SCALE, LOW)
        block = slice(h * rows, (h + 1) * rows)
        log = log_ref[block]
        top = jnp.maximum(log, jnp.max(s, axis=1, keepdims=True))
        weight = jnp.exp2(log - top)
        p = jnp.exp2(s - top).astype(BF)
        value = jnp.dot(
            p, jnp.concatenate([values[h], ones], axis=1), preferred_element_type=F32
        )
        out = (value[:, :WIDTH] + weight * mean_ref[block]) / (value[:, WIDTH:] + weight)
        out = out.astype(BF)
        for j in range(8):
            n = h * 8 + j
            attention_out[:, n * WIDTH : (n + 1) * WIDTH] = out[j * half : (j + 1) * half]


def final(where, queries, cos, sin, up, mean, log, base, ranks):
    half, width = NEW_TOK // 2, queries.shape[1]

    def whole(a):
        return pl.BlockSpec(a.shape, lambda i, w: (0,) * a.ndim)

    rest = [cos, sin, up, mean, log, base, *ranks]
    return pl.pallas_call(
        final_kernel,
        grid_spec=pltpu.PrefetchScalarGridSpec(
            num_scalar_prefetch=1,
            grid=(1,),
            in_specs=[pl.BlockSpec((half, width), lambda i, w: (w[SEQ], 0))]
            + [whole(a) for a in rest],
            out_specs=[
                pl.BlockSpec((half * 4, WIDTH), lambda i, w: (0, 0)),
                pl.BlockSpec((half, width), lambda i, w: (0, 0)),
            ],
            scratch_shapes=[pltpu.VMEM((NEW_TOK * 4, WIDTH), F32)],
        ),
        out_shape=[
            jax.ShapeDtypeStruct((half * 4, WIDTH), BF),
            jax.ShapeDtypeStruct((half, width), BF),
        ],
        compiler_params=pltpu.CompilerParams(vmem_limit_bytes=SMALL_VMEM),
        name="new_kv_and_attention",
    )(where, queries, *rest)


def rotary_tables():
    exponents = jnp.arange(WIDTH // 2, dtype=F32)
    frequency = jnp.exp(exponents * (-2.0 * math.log(500000.0) / WIDTH))
    positions = CACHE + jnp.arange(NEW_TOK, dtype=jnp.int32)
    angles = positions.astype(F32)[:, None] * frequency[None, :]
    cos, sin = jnp.cos(angles), jnp.sin(angles)
    return jnp.concatenate([cos, cos], axis=1), jnp.concatenate([-sin, sin], axis=1)


def flip(axis, mask):
    return lambda a: lax.ppermute(
        a, axis, [(i, i ^ mask) for i in range(lax.axis_size(axis))]
    )


def shift(axis, step):
    size = lax.axis_size(axis)
    return lambda a: lax.ppermute(a, axis, [(i, (i + step) % size) for i in range(size)])


def tie(value, *others):
    return lax.optimization_barrier((value, *others))[0]


def local(
    hidden,
    key_value_weight,
    adapter_down_weight,
    adapter_up_weight,
    queries,
    key_value_cache,
    request_adapter,
):
    seq, group, tensor = (lax.axis_index(a) for a in ("seq", "group", "tensor"))
    place = jnp.stack([seq, seq // 2, seq % 2, tensor, group // 2, group % 2])
    where = jnp.concatenate([place.astype(jnp.int32), request_adapter])

    maps = [adapter_down_weight, adapter_up_weight]
    maps += [flip("group", 1)(a) for a in maps]

    far = [(0, 0, 3, 0, None), (0, 1, 3, 1, None), (0, 2, 4, 0, None)]
    far += [(1, 0, -3, 0, None), (1, 1, -3, 1, None), (1, 2, -4, 1, None)]
    near = [(0, 0, 1, 0, (0, 0)), (0, 1, 1, 1, (0, 1)), (1, 0, 2, 0, (0, 2)), (1, 1, 2, 1, None)]
    near += [(2, 0, -1, 0, (1, 0)), (2, 1, -1, 1, (1, 1))]
    near += [(3, 0, -2, 0, None), (3, 1, -2, 1, (1, 2))]

    sent = relay(where, maps, [], far, "relay_far")
    came = [shift("group", 4)(sent[0]), shift("group", -4)(sent[1])]

    cache_rows = key_value_cache.reshape(-1, WIDTH)
    *parts, cache_rows, queries = prep(
        tie(where, *sent), hidden, key_value_weight.reshape(-1, WIDTH), cache_rows, queries
    )
    received = [shift("tensor", step)(parts[step]) for step in (1, 2, 3)]
    o2, o3 = attend(tie(where, parts[0]), queries, cache_rows, True)

    sent = relay(tie(where, o2), maps, came, near, "relay_near")
    came = [shift("group", 2 * hops)(a) for hops, a in zip((1, 2, -1, -2), sent)]
    received = lax.optimization_barrier((*received, *sent))[:3]
    base = (parts[0].astype(F32) + sum(r.astype(F32) for r in received)).astype(BF)
    got2 = flip("seq", 2)(tie(o2, *sent))
    o0, o1 = attend(tie(where, *sent, base), queries, cache_rows, False)

    cos, sin = rotary_tables()
    mine, others = rank_parts(tie(where, o1, cos, sin, got2), hidden, base, maps, came)
    rank, base, ups = seq_sum(
        where, [mine, flip("seq", 1)(mine), flip("seq", 2)(others), flip("seq", 3)(others)]
    )
    got1, got3 = flip("seq", 1)(tie(o1, rank)), flip("seq", 3)(tie(o3, rank))
    ranks = [rank] + [shift("tensor", step)(rank) for step in (1, 2, 3)]
    mean, log = merge(list(lax.optimization_barrier((o0, got1, got2, got3, rank)))[:4])

    new_kv, attention = final(where, queries, cos, sin, ups, mean, log, base, ranks)
    return new_kv.reshape(-1, 2, 2, WIDTH), attention


def solution(mesh):
    in_specs = (
        P("group", ("tensor", "seq")),
        P(("tensor", "seq"), None, None, None),
        P("group", ("tensor", "seq"), None),
        P("group", None, None, "tensor"),
        P("group", "tensor"),
        P("group", "seq", "tensor", None, None),
        P(),
    )
    out_specs = (P(("group", "seq"), "tensor", None, None), P(("group", "seq"), "tensor"))
    return jax.shard_map(local, mesh=mesh, in_specs=in_specs, out_specs=out_specs, check_vma=False)
```

profile of v0, /device:TPU:32, one launch (start us, length us, event | category | flops | bytes accessed | tf_op | source)
XLA Modules:
  0.0 87.9 jit_solution(5712526976567540258)
XLA Ops:
  0.6 0.1 collective-permute-start
  0.7 0.5 collective-permute-start.1
  1.2 0.7 concatenate.9.where
  2.0 0.3 fusion
  2.3 0.1 pad_maximum_fusion
  2.4 0.8 collective-permute-done.1.refs_3_
  3.2 0.0 collective-permute-done.refs_2_
  3.2 0.9 relay_far.1
  4.1 3.3 %collective-permute-start.2 = (bf16[3,576,128]{2,1,0:T(8,128)(2,1)S(1)}, bf16[3,576,128]{2,1,0:T(8,128)(2,1)S(1)}, u32[]{:S(2)}, u32[]{:S(2)}) collective-permute-start(bf16[3,576,128]{2,1,0:T(8,128)(2,1)S(1)} %get-tuple-element.42), channel_id=1, source_target_pairs={{0,64},{16,80},{32,96},{48,112},{64,128},{80,144},{96,160},{112,17... | collective-permute-start | bytes 1327112 | tf_op jit(solution)/shard_map/ppermute | solution.py:512
  7.4 2.2 %collective-permute-start.3 = (bf16[3,576,128]{2,1,0:T(8,128)(2,1)S(1)}, bf16[3,576,128]{2,1,0:T(8,128)(2,1)S(1)}, u32[]{:S(2)}, u32[]{:S(2)}) collective-permute-start(bf16[3,576,128]{2,1,0:T(8,128)(2,1)S(1)} %get-tuple-element.43), channel_id=1, source_target_pairs={{0,192},{16,208},{32,224},{48,240},{64,0},{80,16},{96,32},{112,48}... | collective-permute-start | bytes 1327112 | tf_op jit(solution)/shard_map/ppermute | solution.py:512
  9.7 5.0 %base_partial.1 = (bf16[256,512]{1,0:T(8,128)(2,1)S(1)}, bf16[256,512]{1,0:T(8,128)(2,1)S(1)}, bf16[256,512]{1,0:T(8,128)(2,1)S(1)}, bf16[256,512]{1,0:T(8,128)(...) custom-call(s32[38]{0:T(128)S(1)} %concatenate.9.where, bf16[256,512]{1,0:T(8,128)(2,1)} %hidden_ref.1, ...), custom_call_target="tpu_custom_call" | custom-call | flops 536870912 | bytes 11534336 | tf_op jit(solution)/shard_map/base_partial/pallas_call | solution.py:78
  14.7 1.6 %collective-permute-start.4 = (bf16[256,512]{1,0:T(8,128)(2,1)S(1)}, bf16[256,512]{1,0:T(8,128)(2,1)S(1)}, u32[]{:S(2)}, u32[]{:S(2)}) collective-permute-start(bf16[256,512]{1,0:T(8,128)(2,1)S(1)} %get-tuple-element.55), channel_id=1, source_target_pairs={{0,4},{4,8},{8,12},{12,0},{1,5},{5,9},{9,13},{13,1},{2,6},{6,10},{... | collective-permute-start | bytes 786440 | tf_op jit(solution)/shard_map/ppermute | solution.py:512
  16.2 2.7 %collective-permute-start.5 = (bf16[256,512]{1,0:T(8,128)(2,1)S(1)}, bf16[256,512]{1,0:T(8,128)(2,1)S(1)}, u32[]{:S(2)}, u32[]{:S(2)}) collective-permute-start(bf16[256,512]{1,0:T(8,128)(2,1)S(1)} %get-tuple-element.56), channel_id=1, source_target_pairs={{0,8},{4,12},{8,0},{12,4},{1,9},{5,13},{9,1},{13,5},{2,10},{6,14},... | collective-permute-start | bytes 786440 | tf_op jit(solution)/shard_map/ppermute | solution.py:512
  19.0 1.4 %collective-permute-start.6 = (bf16[256,512]{1,0:T(8,128)(2,1)S(1)}, bf16[256,512]{1,0:T(8,128)(2,1)S(1)}, u32[]{:S(2)}, u32[]{:S(2)}) collective-permute-start(bf16[256,512]{1,0:T(8,128)(2,1)S(1)} %get-tuple-element.57), channel_id=1, source_target_pairs={{0,12},{4,0},{8,4},{12,8},{1,13},{5,1},{9,5},{13,9},{2,14},{6,2},{... | collective-permute-start | bytes 786440 | tf_op jit(solution)/shard_map/ppermute | solution.py:512
  20.4 12.6 %attend_other.1 = (bf16[64,2176]{1,0:T(8,128)(2,1)S(1)}, bf16[64,2176]{1,0:T(8,128)(2,1)S(1)}) custom-call(s32[38]{0:T(128)S(1)} %concatenate.9.where, bf16[256,2048]{1,0:T(8,128)(2,1)S(1)} %get-tuple-element.45.q_ref, bf16[32768,128]{1,0:T(8,128)(2,1)S(1)} %get-tuple-element.48.x_ref), custom_call_target="tpu_custom_call" | custom-call | flops 8589934592 | bytes 5242880 | tf_op jit(solution)/shard_map/attend_other/pallas_call | solution.py:190
  33.0 0.0 collective-permute-done.2.refs_4_
  33.0 0.0 collective-permute-done.3.refs_5_
  33.0 1.9 %relay_near.1 = (bf16[2,576,128]{2,1,0:T(8,128)(2,1)S(1)}, bf16[2,576,128]{2,1,0:T(8,128)(2,1)S(1)}, bf16[2,576,128]{2,1,0:T(8,128)(2,1)S(1)}, bf16[2,576,128]{2,1,0:T(8,128)(2,1)S(1)}) custom-call(s32[38]{0:T(128)S(1)} %concatenate.9.where, bf16[4,512,128]{2,1,0:T(8,128)(2,1)} %refs_0_.5, bf16[4,2,64,256]{3,2,1,0:T(8,128)(2,1)} %refs_1_.5, ...), custom_call_target="tpu_custom_call" | custom-call | bytes 2097152 | tf_op jit(solution)/shard_map/relay_near/pallas_call | solution.py:283
  35.0 0.2 collective-permute-start.10
  35.2 3.0 %collective-permute-start.11 = (bf16[2,576,128]{2,1,0:T(8,128)(2,1)S(1)}, bf16[2,576,128]{2,1,0:T(8,128)(2,1)S(1)}, u32[]{:S(2)}, u32[]{:S(2)}) collective-permute-start(bf16[2,576,128]{2,1,0:T(8,128)(2,1)S(1)} %get-tuple-element.54), channel_id=1, source_target_pairs={{0,192},{16,208},{32,224},{48,240},{64,0},{80,16},{96,32},{112,48}... | collective-permute-start | bytes 884744 | tf_op jit(solution)/shard_map/ppermute | solution.py:512
  38.2 0.0 collective-permute-done.4
  38.2 0.9 collective-permute-start.8
  39.0 0.0 collective-permute-done.5
  39.0 2.2 %collective-permute-start.9 = (bf16[2,576,128]{2,1,0:T(8,128)(2,1)S(1)}, bf16[2,576,128]{2,1,0:T(8,128)(2,1)S(1)}, u32[]{:S(2)}, u32[]{:S(2)}) collective-permute-start(bf16[2,576,128]{2,1,0:T(8,128)(2,1)S(1)} %get-tuple-element.52), channel_id=1, source_target_pairs={{0,64},{16,80},{32,96},{48,112},{64,128},{80,144},{96,160},{112,17... | collective-permute-start | bytes 884744 | tf_op jit(solution)/shard_map/ppermute | solution.py:512
  41.2 0.0 collective-permute-done.6
  41.2 3.2 %collective-permute-start.7 = (bf16[64,2176]{1,0:T(8,128)(2,1)S(1)}, bf16[64,2176]{1,0:T(8,128)(2,1)S(1)}, u32[]{:S(2)}, u32[]{:S(2)}) collective-permute-start(bf16[64,2176]{1,0:T(8,128)(2,1)S(1)} %get-tuple-element.63), channel_id=1, source_target_pairs={{0,2},{1,3},{2,0},{3,1},{4,6},{5,7},{6,4},{7,5},{8,10},{9,11},{10,... | collective-permute-start | bytes 835592 | tf_op jit(solution)/shard_map/ppermute | solution.py:505
  44.4 0.1 add_convert_fusion.base_ref
  44.5 0.0 copy-start
  44.6 12.6 %attend_own.1 = (bf16[64,2176]{1,0:T(8,128)(2,1)S(1)}, bf16[64,2176]{1,0:T(8,128)(2,1)S(1)}) custom-call(s32[38]{0:T(128)S(1)} %concatenate.9.where, bf16[256,2048]{1,0:T(8,128)(2,1)S(1)} %get-tuple-element.45.q_ref, bf16[32768,128]{1,0:T(8,128)(2,1)S(1)} %get-tuple-element.48.x_ref), custom_call_target="tpu_custom_call" | custom-call | flops 8589934592 | bytes 5242880 | tf_op jit(solution)/shard_map/attend_own/pallas_call | solution.py:190
  57.1 0.0 collective-permute-done.7.refs_2_
  57.2 0.0 collective-permute-done.10.refs_6_
  57.2 0.0 collective-permute-done.11.refs_7_
  57.2 0.0 collective-permute-done.8.refs_4_
  57.2 5.1 %collective-permute-done.9.refs_5_ = bf16[2,576,128]{2,1,0:T(8,128)(2,1)S(1)} collective-permute-done((bf16[2,576,128]{2,1,0:T(8,128)(2,1)S(1)}, bf16[2,576,128]{2,1,0:T(8,128)(2,1)S(1)}, u32[]{:S(2)}, u32[]{:S(2)}) %collective-permute-start.9) | collective-permute-done | bytes 294944 | tf_op jit(solution)/shard_map/ppermute | solution.py:512
  62.2 0.0 copy-done
  62.3 1.2 %rank_partial.1 = (bf16[704,128]{1,0:T(8,128)(2,1)S(1)}, bf16[704,128]{1,0:T(8,128)(2,1)S(1)}) custom-call(s32[38]{0:T(128)S(1)} %concatenate.9.where, bf16[256,512]{1,0:T(8,128)(2,1)S(1)} %copy-done, bf16[256,512]{1,0:T(8,128)(2,1)S(1)} %add_convert_fusion.base_ref, bf16[4,512,128]{2,1,0:T(8,128)(2,1)} %refs_0_.5, bf16[4,2,64,256]{3,2,1,0:T(8,128)(2,1)} %refs_1_.5, ...), custom_call_target="tpu_custom_call" | custom-call | tf_op jit(solution)/shard_map/rank_partial/pallas_call | solution.py:347
  63.4 1.7 %collective-permute-start.12 = (bf16[704,128]{1,0:T(8,128)(2,1)S(1)}, bf16[704,128]{1,0:T(8,128)(2,1)S(1)}, u32[]{:S(2)}, u32[]{:S(2)}) collective-permute-start(bf16[704,128]{1,0:T(8,128)(2,1)S(1)} %get-tuple-element.65.refs_0_), channel_id=1, source_target_pairs={{0,1},{1,0},{2,3},{3,2},{4,5},{5,4},{6,7},{7,6},{8,9},{9,8},{10,11... | collective-permute-start | bytes 540680 | tf_op jit(solution)/shard_map/ppermute | solution.py:505
  65.1 2.9 %collective-permute-start.13 = (bf16[704,128]{1,0:T(8,128)(2,1)S(1)}, bf16[704,128]{1,0:T(8,128)(2,1)S(1)}, u32[]{:S(2)}, u32[]{:S(2)}) collective-permute-start(bf16[704,128]{1,0:T(8,128)(2,1)S(1)} %get-tuple-element.66), channel_id=1, source_target_pairs={{0,2},{1,3},{2,0},{3,1},{4,6},{5,7},{6,4},{7,5},{8,10},{9,11},{10,... | collective-permute-start | bytes 540680 | tf_op jit(solution)/shard_map/ppermute | solution.py:505
  68.0 0.2 collective-permute-start.14
  68.2 2.1 %collective-permute-done.12.refs_1_ = bf16[704,128]{1,0:T(8,128)(2,1)S(1)} collective-permute-done((bf16[704,128]{1,0:T(8,128)(2,1)S(1)}, bf16[704,128]{1,0:T(8,128)(2,1)S(1)}, u32[]{:S(2)}, u32[]{:S(2)}) %collective-permute-start.12) | collective-permute-done | bytes 180256 | tf_op jit(solution)/shard_map/ppermute | solution.py:505
  70.3 4.1 %collective-permute-done.13.refs_2_ = bf16[704,128]{1,0:T(8,128)(2,1)S(1)} collective-permute-done((bf16[704,128]{1,0:T(8,128)(2,1)S(1)}, bf16[704,128]{1,0:T(8,128)(2,1)S(1)}, u32[]{:S(2)}, u32[]{:S(2)}) %collective-permute-start.13) | collective-permute-done | bytes 180256 | tf_op jit(solution)/shard_map/ppermute | solution.py:505
  74.4 1.8 %collective-permute-done.14.refs_3_ = bf16[704,128]{1,0:T(8,128)(2,1)S(1)} collective-permute-done((bf16[704,128]{1,0:T(8,128)(2,1)S(1)}, bf16[704,128]{1,0:T(8,128)(2,1)S(1)}, u32[]{:S(2)}, u32[]{:S(2)}) %collective-permute-start.14) | collective-permute-done | bytes 180256 | tf_op jit(solution)/shard_map/ppermute | solution.py:505
  76.2 0.6 seq_sum.1
  76.9 0.7 collective-permute-start.16
  77.6 0.0 collective-permute-start.15
  77.6 0.6 collective-permute-start.17
  78.2 1.0 %collective-permute-start.18 = (bf16[128,128]{1,0:T(8,128)(2,1)S(1)}, bf16[128,128]{1,0:T(8,128)(2,1)S(1)}, u32[]{:S(2)}, u32[]{:S(2)}) collective-permute-start(bf16[128,128]{1,0:T(8,128)(2,1)S(1)} %get-tuple-element.69.rest_0_), channel_id=1, source_target_pairs={{0,8},{4,12},{8,0},{12,4},{1,9},{5,13},{9,1},{13,5},{2,10},{6,14},... | collective-permute-start | bytes 98312 | tf_op jit(solution)/shard_map/ppermute | solution.py:512
  79.1 1.7 %collective-permute-start.19 = (bf16[128,128]{1,0:T(8,128)(2,1)S(1)}, bf16[128,128]{1,0:T(8,128)(2,1)S(1)}, u32[]{:S(2)}, u32[]{:S(2)}) collective-permute-start(bf16[128,128]{1,0:T(8,128)(2,1)S(1)} %get-tuple-element.69.rest_0_), channel_id=1, source_target_pairs={{0,12},{4,0},{8,4},{12,8},{1,13},{5,1},{9,5},{13,9},{2,14},{6,2},{... | collective-permute-start | bytes 98312 | tf_op jit(solution)/shard_map/ppermute | solution.py:512
  80.8 3.9 %collective-permute-done.16.refs_3_ = bf16[64,2176]{1,0:T(8,128)(2,1)S(1)} collective-permute-done((bf16[64,2176]{1,0:T(8,128)(2,1)S(1)}, bf16[64,2176]{1,0:T(8,128)(2,1)S(1)}, u32[]{:S(2)}, u32[]{:S(2)}) %collective-permute-start.16) | collective-permute-done | bytes 278560 | tf_op jit(solution)/shard_map/ppermute | solution.py:505
  84.7 0.0 collective-permute-done.15.refs_1_
  84.7 0.9 %merge_prefix.1 = (f32[1024,128]{1,0:T(8,128)S(1)}, f32[1024,128]{1,0:T(8,128)S(1)}) custom-call(bf16[64,2176]{1,0:T(8,128)(2,1)S(1)} %get-tuple-element.73.refs_0_, bf16[64,2176]{1,0:T(8,128)(2,1)S(1)} %collective-permute-done.15.refs_1_, bf16[64,2176]{1,0:T(8,128)(2,1)S(1)} %collective-permute-done.7.refs_2_, ...), custom_call_target="tpu_custom_call" | custom-call | tf_op jit(solution)/shard_map/merge_prefix/pallas_call | solution.py:413
  85.6 0.0 collective-permute-done.17.rest_1_
  85.6 0.0 collective-permute-done.18.rest_2_
  85.7 0.0 collective-permute-done.19.rest_3_
  85.7 2.2 %new_kv_and_attention.1 = (bf16[256,128]{1,0:T(8,128)(2,1)}, bf16[64,2048]{1,0:T(8,128)(2,1)}) custom-call(s32[38]{0:T(128)S(1)} %concatenate.9.where, bf16[256,2048]{1,0:T(8,128)(2,1)S(1)} %get-tuple-element.45.q_ref, f32[128,128]{1,0:T(8,128)S(1)} %get-tuple-element.85.cos_ref, f32[128,128]{1,0:T(8,128)S(1)} %get-tuple-element.86.sin_ref, ...), custom_call_target="tpu_custom_call" | custom-call | tf_op jit(solution)/shard_map/new_kv_and_attention/pallas_call | solution.py:473
  (2 shorter events, 0.0 us)
Async XLA Ops:
  0.6 2.6 %collective-permute-start = (bf16[4,512,128]{2,1,0:T(8,128)(2,1)}, bf16[4,512,128]{2,1,0:T(8,128)(2,1)S(1)}, u32[]{:S(2)}, u32[]{:S(2)}) collective-permute-start(bf16[4,512,128]{2,1,0:T(8,128)(2,1)} %refs_0_.5), channel_id=1, source_target_pairs={{0,16},{16,0},{32,48},{48,32},{64,80},{80,64},{96,112},{112,96},{1... | collective-permute-start | bytes 1572872 | tf_op jit(solution)/shard_map/ppermute | solution.py:505
  0.7 2.5 %collective-permute-start.1 = (bf16[4,2,64,256]{3,2,1,0:T(8,128)(2,1)}, bf16[4,2,64,256]{3,2,1,0:T(8,128)(2,1)S(1)}, u32[]{:S(2)}, u32[]{:S(2)}) collective-permute-start(bf16[4,2,64,256]{3,2,1,0:T(8,128)(2,1)} %refs_1_.5), channel_id=1, source_target_pairs={{0,16},{16,0},{32,48},{48,32},{64,80},{80,64},{96,112},{112,96},{1... | collective-permute-start | bytes 786440 | tf_op jit(solution)/shard_map/ppermute | solution.py:505
  4.1 28.9 %collective-permute-start.2 = (bf16[3,576,128]{2,1,0:T(8,128)(2,1)S(1)}, bf16[3,576,128]{2,1,0:T(8,128)(2,1)S(1)}, u32[]{:S(2)}, u32[]{:S(2)}) collective-permute-start(bf16[3,576,128]{2,1,0:T(8,128)(2,1)S(1)} %get-tuple-element.42), channel_id=1, source_target_pairs={{0,64},{16,80},{32,96},{48,112},{64,128},{80,144},{96,160},{112,17... | collective-permute-start | bytes 1327112 | tf_op jit(solution)/shard_map/ppermute | solution.py:512
  7.4 25.6 %collective-permute-start.3 = (bf16[3,576,128]{2,1,0:T(8,128)(2,1)S(1)}, bf16[3,576,128]{2,1,0:T(8,128)(2,1)S(1)}, u32[]{:S(2)}, u32[]{:S(2)}) collective-permute-start(bf16[3,576,128]{2,1,0:T(8,128)(2,1)S(1)} %get-tuple-element.43), channel_id=1, source_target_pairs={{0,192},{16,208},{32,224},{48,240},{64,0},{80,16},{96,32},{112,48}... | collective-permute-start | bytes 1327112 | tf_op jit(solution)/shard_map/ppermute | solution.py:512
  14.7 23.5 %collective-permute-start.4 = (bf16[256,512]{1,0:T(8,128)(2,1)S(1)}, bf16[256,512]{1,0:T(8,128)(2,1)S(1)}, u32[]{:S(2)}, u32[]{:S(2)}) collective-permute-start(bf16[256,512]{1,0:T(8,128)(2,1)S(1)} %get-tuple-element.55), channel_id=1, source_target_pairs={{0,4},{4,8},{8,12},{12,0},{1,5},{5,9},{9,13},{13,1},{2,6},{6,10},{... | collective-permute-start | bytes 786440 | tf_op jit(solution)/shard_map/ppermute | solution.py:512
  16.2 22.8 %collective-permute-start.5 = (bf16[256,512]{1,0:T(8,128)(2,1)S(1)}, bf16[256,512]{1,0:T(8,128)(2,1)S(1)}, u32[]{:S(2)}, u32[]{:S(2)}) collective-permute-start(bf16[256,512]{1,0:T(8,128)(2,1)S(1)} %get-tuple-element.56), channel_id=1, source_target_pairs={{0,8},{4,12},{8,0},{12,4},{1,9},{5,13},{9,1},{13,5},{2,10},{6,14},... | collective-permute-start | bytes 786440 | tf_op jit(solution)/shard_map/ppermute | solution.py:512
  19.0 22.3 %collective-permute-start.6 = (bf16[256,512]{1,0:T(8,128)(2,1)S(1)}, bf16[256,512]{1,0:T(8,128)(2,1)S(1)}, u32[]{:S(2)}, u32[]{:S(2)}) collective-permute-start(bf16[256,512]{1,0:T(8,128)(2,1)S(1)} %get-tuple-element.57), channel_id=1, source_target_pairs={{0,12},{4,0},{8,4},{12,8},{1,13},{5,1},{9,5},{13,9},{2,14},{6,2},{... | collective-permute-start | bytes 786440 | tf_op jit(solution)/shard_map/ppermute | solution.py:512
  35.0 22.2 %collective-permute-start.10 = (bf16[2,576,128]{2,1,0:T(8,128)(2,1)S(1)}, bf16[2,576,128]{2,1,0:T(8,128)(2,1)S(1)}, u32[]{:S(2)}, u32[]{:S(2)}) collective-permute-start(bf16[2,576,128]{2,1,0:T(8,128)(2,1)S(1)} %get-tuple-element.53), channel_id=1, source_target_pairs={{0,224},{16,240},{32,0},{48,16},{64,32},{80,48},{96,64},{112,80},{... | collective-permute-start | bytes 884744 | tf_op jit(solution)/shard_map/ppermute | solution.py:512
  35.2 22.0 %collective-permute-start.11 = (bf16[2,576,128]{2,1,0:T(8,128)(2,1)S(1)}, bf16[2,576,128]{2,1,0:T(8,128)(2,1)S(1)}, u32[]{:S(2)}, u32[]{:S(2)}) collective-permute-start(bf16[2,576,128]{2,1,0:T(8,128)(2,1)S(1)} %get-tuple-element.54), channel_id=1, source_target_pairs={{0,192},{16,208},{32,224},{48,240},{64,0},{80,16},{96,32},{112,48}... | collective-permute-start | bytes 884744 | tf_op jit(solution)/shard_map/ppermute | solution.py:512
  38.2 19.0 %collective-permute-start.8 = (bf16[2,576,128]{2,1,0:T(8,128)(2,1)S(1)}, bf16[2,576,128]{2,1,0:T(8,128)(2,1)S(1)}, u32[]{:S(2)}, u32[]{:S(2)}) collective-permute-start(bf16[2,576,128]{2,1,0:T(8,128)(2,1)S(1)} %get-tuple-element.51), channel_id=1, source_target_pairs={{0,32},{16,48},{32,64},{48,80},{64,96},{80,112},{96,128},{112,144}... | collective-permute-start | bytes 884744 | tf_op jit(solution)/shard_map/ppermute | solution.py:512
  39.0 23.2 %collective-permute-start.9 = (bf16[2,576,128]{2,1,0:T(8,128)(2,1)S(1)}, bf16[2,576,128]{2,1,0:T(8,128)(2,1)S(1)}, u32[]{:S(2)}, u32[]{:S(2)}) collective-permute-start(bf16[2,576,128]{2,1,0:T(8,128)(2,1)S(1)} %get-tuple-element.52), channel_id=1, source_target_pairs={{0,64},{16,80},{32,96},{48,112},{64,128},{80,144},{96,160},{112,17... | collective-permute-start | bytes 884744 | tf_op jit(solution)/shard_map/ppermute | solution.py:512
  41.2 15.9 %collective-permute-start.7 = (bf16[64,2176]{1,0:T(8,128)(2,1)S(1)}, bf16[64,2176]{1,0:T(8,128)(2,1)S(1)}, u32[]{:S(2)}, u32[]{:S(2)}) collective-permute-start(bf16[64,2176]{1,0:T(8,128)(2,1)S(1)} %get-tuple-element.63), channel_id=1, source_target_pairs={{0,2},{1,3},{2,0},{3,1},{4,6},{5,7},{6,4},{7,5},{8,10},{9,11},{10,... | collective-permute-start | bytes 835592 | tf_op jit(solution)/shard_map/ppermute | solution.py:505
  44.5 17.7 %copy-start = (bf16[256,512]{1,0:T(8,128)(2,1)S(1)}, bf16[256,512]{1,0:T(8,128)(2,1)}, u32[]{:S(2)}) copy-start(bf16[256,512]{1,0:T(8,128)(2,1)} %hidden_ref.1) | copy-start | bytes 786436
  63.4 6.9 %collective-permute-start.12 = (bf16[704,128]{1,0:T(8,128)(2,1)S(1)}, bf16[704,128]{1,0:T(8,128)(2,1)S(1)}, u32[]{:S(2)}, u32[]{:S(2)}) collective-permute-start(bf16[704,128]{1,0:T(8,128)(2,1)S(1)} %get-tuple-element.65.refs_0_), channel_id=1, source_target_pairs={{0,1},{1,0},{2,3},{3,2},{4,5},{5,4},{6,7},{7,6},{8,9},{9,8},{10,11... | collective-permute-start | bytes 540680 | tf_op jit(solution)/shard_map/ppermute | solution.py:505
  65.1 9.3 %collective-permute-start.13 = (bf16[704,128]{1,0:T(8,128)(2,1)S(1)}, bf16[704,128]{1,0:T(8,128)(2,1)S(1)}, u32[]{:S(2)}, u32[]{:S(2)}) collective-permute-start(bf16[704,128]{1,0:T(8,128)(2,1)S(1)} %get-tuple-element.66), channel_id=1, source_target_pairs={{0,2},{1,3},{2,0},{3,1},{4,6},{5,7},{6,4},{7,5},{8,10},{9,11},{10,... | collective-permute-start | bytes 540680 | tf_op jit(solution)/shard_map/ppermute | solution.py:505
  68.0 8.3 %collective-permute-start.14 = (bf16[704,128]{1,0:T(8,128)(2,1)S(1)}, bf16[704,128]{1,0:T(8,128)(2,1)S(1)}, u32[]{:S(2)}, u32[]{:S(2)}) collective-permute-start(bf16[704,128]{1,0:T(8,128)(2,1)S(1)} %get-tuple-element.66), channel_id=1, source_target_pairs={{0,3},{1,2},{2,1},{3,0},{4,7},{5,6},{6,5},{7,4},{8,11},{9,10},{10,... | collective-permute-start | bytes 540680 | tf_op jit(solution)/shard_map/ppermute | solution.py:505
  76.9 7.8 %collective-permute-start.16 = (bf16[64,2176]{1,0:T(8,128)(2,1)S(1)}, bf16[64,2176]{1,0:T(8,128)(2,1)S(1)}, u32[]{:S(2)}, u32[]{:S(2)}) collective-permute-start(bf16[64,2176]{1,0:T(8,128)(2,1)S(1)} %get-tuple-element.72), channel_id=1, source_target_pairs={{0,3},{1,2},{2,1},{3,0},{4,7},{5,6},{6,5},{7,4},{8,11},{9,10},{10,... | collective-permute-start | bytes 835592 | tf_op jit(solution)/shard_map/ppermute | solution.py:505
  77.6 7.2 %collective-permute-start.15 = (bf16[64,2176]{1,0:T(8,128)(2,1)S(1)}, bf16[64,2176]{1,0:T(8,128)(2,1)S(1)}, u32[]{:S(2)}, u32[]{:S(2)}) collective-permute-start(bf16[64,2176]{1,0:T(8,128)(2,1)S(1)} %get-tuple-element.70), channel_id=1, source_target_pairs={{0,1},{1,0},{2,3},{3,2},{4,5},{5,4},{6,7},{7,6},{8,9},{9,8},{10,11... | collective-permute-start | bytes 835592 | tf_op jit(solution)/shard_map/ppermute | solution.py:505
  77.6 8.1 %collective-permute-start.17 = (bf16[128,128]{1,0:T(8,128)(2,1)S(1)}, bf16[128,128]{1,0:T(8,128)(2,1)S(1)}, u32[]{:S(2)}, u32[]{:S(2)}) collective-permute-start(bf16[128,128]{1,0:T(8,128)(2,1)S(1)} %get-tuple-element.69.rest_0_), channel_id=1, source_target_pairs={{0,4},{4,8},{8,12},{12,0},{1,5},{5,9},{9,13},{13,1},{2,6},{6,10},{... | collective-permute-start | bytes 98312 | tf_op jit(solution)/shard_map/ppermute | solution.py:512
  78.2 7.5 %collective-permute-start.18 = (bf16[128,128]{1,0:T(8,128)(2,1)S(1)}, bf16[128,128]{1,0:T(8,128)(2,1)S(1)}, u32[]{:S(2)}, u32[]{:S(2)}) collective-permute-start(bf16[128,128]{1,0:T(8,128)(2,1)S(1)} %get-tuple-element.69.rest_0_), channel_id=1, source_target_pairs={{0,8},{4,12},{8,0},{12,4},{1,9},{5,13},{9,1},{13,5},{2,10},{6,14},... | collective-permute-start | bytes 98312 | tf_op jit(solution)/shard_map/ppermute | solution.py:512
  79.1 6.5 %collective-permute-start.19 = (bf16[128,128]{1,0:T(8,128)(2,1)S(1)}, bf16[128,128]{1,0:T(8,128)(2,1)S(1)}, u32[]{:S(2)}, u32[]{:S(2)}) collective-permute-start(bf16[128,128]{1,0:T(8,128)(2,1)S(1)} %get-tuple-element.69.rest_0_), channel_id=1, source_target_pairs={{0,12},{4,0},{8,4},{12,8},{1,13},{5,1},{9,5},{13,9},{2,14},{6,2},{... | collective-permute-start | bytes 98312 | tf_op jit(solution)/shard_map/ppermute | solution.py:512
where the time goes:
time: 87.1 us; the launch traced here: 87.9 us
  Pallas kernels  37.9 us (44%)
  starting transfers between devices  30.1 us (35%)
  waiting for transfers between devices  17.8 us (20%)
    pallas_call x2, Pallas kernels, attend(): pl.pallas_call(attend_kernel, grid_spec=pltpu.PrefetchScalarGridSpec(num_...  25.2 us
    ppermute x12, starting transfers between devices, shift(): lax.ppermute(a, axis, [(i, (i + step) % size) for i in range(size)])  20.8 us
    ppermute x8, waiting for transfers between devices, flip(): lax.ppermute(a, axis, [(i, i ^ mask) for i in range(lax.axis_size(axis))])  12.7 us
    ppermute x8, starting transfers between devices, flip(): lax.ppermute(a, axis, [(i, i ^ mask) for i in range(lax.axis_size(axis))])  9.25 us
    ppermute x12, waiting for transfers between devices, shift(): lax.ppermute(a, axis, [(i, (i + step) % size) for i in range(size)])  5.09 us
    pallas_call x1, Pallas kernels, prep(): pl.pallas_call(prep_kernel, in_specs=[pl.BlockSpec(memory_space=pltpu.SME...  4.99 us
    pallas_call x2, Pallas kernels, relay(): pl.pallas_call(functools.partial(relay_kernel, slots, len(came)), in_spec...  2.81 us
    pallas_call x1, Pallas kernels, final(): pl.pallas_call(final_kernel, grid_spec=pltpu.PrefetchScalarGridSpec(num_s...  2.22 us
  transfers between devices with their start and end apart: 20, of which 6 were waited for; matrix products, arithmetic and copies ran while one was open for 1% of the time, Pallas kernels for 38%

commit v1 on v0

--- a/solution.py
+++ b/solution.py
@@ -294,10 +294,9 @@
     )(where, *map(in_hbm, maps[:2]), *maps[2:], *came)
 
 
-def rank_kernel(where, hidden_ref, base_ref, *refs):
-    maps, came, (mine_out, others_out, held, sem) = refs[:4], refs[4:8], refs[8:]
+def rank_kernel(where, hidden_ref, *refs):
+    maps, came, (rank_out, up_out, held, sem) = refs[:4], refs[4:8], refs[8:]
     depth = hidden_ref.shape[1]
-    height = held.shape[1] - depth
     waits = []
     for r in range(2):
         adapter = owner(where, where[PLANE], r)
@@ -323,67 +322,67 @@
             def _(r=r, source=source):
                 held[r] = source[r]
 
-    half = where[HALF]
-    for out, request in ((mine_out, half), (others_out, 1 - half)):
-        rows = pl.ds(pl.multiple_of(request * NEW_TOK, NEW_TOK), NEW_TOK)
-        for part in range(4):
-            start = NEW_TOK + height + part * NEW_TOK
-            out[start : start + NEW_TOK] = base_ref[rows, part * WIDTH : (part + 1) * WIDTH]
-    for wait in waits:
-        wait()
-    for out, request in ((mine_out, half), (others_out, 1 - half)):
-        rows = pl.ds(pl.multiple_of(request * NEW_TOK, NEW_TOK), NEW_TOK)
-        out[:NEW_TOK] = jnp.dot(
-            hidden_ref[rows], held[request, :depth], preferred_element_type=F32
+    for r in range(2):
+        waits[r]()
+        rank_out[r * NEW_TOK : (r + 1) * NEW_TOK] = jnp.dot(
+            hidden_ref[r * NEW_TOK : (r + 1) * NEW_TOK],
+            held[r, :depth],
+            preferred_element_type=F32,
         ).astype(BF)
-        out[NEW_TOK : NEW_TOK + height] = held[request, depth:]
-
-
-def rank_parts(where, hidden, base, maps, came):
+        up_out[r] = held[r, depth:]
+
+
+def rank_parts(where, hidden, maps, came):
     height = came[0].shape[1]
-    out = jax.ShapeDtypeStruct((5 * NEW_TOK + height - hidden.shape[1], WIDTH), BF)
     anywhere = pl.BlockSpec(memory_space=pl.ANY)
     whole = pl.BlockSpec(memory_space=pltpu.VMEM)
     return pl.pallas_call(
         rank_kernel,
-        in_specs=[pl.BlockSpec(memory_space=pltpu.SMEM), whole, whole]
+        in_specs=[pl.BlockSpec(memory_space=pltpu.SMEM), whole]
         + [anywhere] * 4
         + [whole] * 4,
         out_specs=[whole, whole],
-        out_shape=[out, out],
+        out_shape=[
+            jax.ShapeDtypeStruct((hidden.shape[0], WIDTH), BF),
+            jax.ShapeDtypeStruct((2, height - hidden.shape[1], WIDTH), BF),
+        ],
         scratch_shapes=[pltpu.VMEM((2, height, WIDTH), BF), pltpu.SemaphoreType.DMA((2, 2))],
         compiler_params=pltpu.CompilerParams(vmem_limit_bytes=SMALL_VMEM),
         name="rank_partial",
-    )(where, hidden, base, *map(in_hbm, maps[:2]), *maps[2:], *came)
-
-
-def seq_kernel(where, *refs):
-    parts, (rank_out, base_out, up_out) = refs[:4], refs[4:]
-    after = NEW_TOK + up_out.shape[1]
-    rank_out[...] = sum(part[:NEW_TOK].astype(F32) for part in parts).astype(BF)
-    for step, part in enumerate(parts):
-        up_out[jnp.bitwise_xor(where[SEQ], step)] = part[NEW_TOK:after]
-    for col in range(4):
-        start = after + col * NEW_TOK
-        base_out[:, col * WIDTH : (col + 1) * WIDTH] = sum(
-            part[start : start + NEW_TOK].astype(F32) for part in parts
-        )
-
-
-def seq_sum(where, parts):
+    )(where, hidden, *map(in_hbm, maps[:2]), *maps[2:], *came)
+
+
+def parcel_kernel(where, base_ref, got_ref, up_ref, *refs):
+    ranks, outs = refs[:4], refs[4:]
+    after = NEW_TOK + up_ref.shape[1]
+    half = where[HALF]
+    for out, request in zip(outs, (half, 1 - half)):
+        rows = pl.ds(pl.multiple_of(request * NEW_TOK, NEW_TOK), NEW_TOK)
+        out[:NEW_TOK] = sum(rank[rows].astype(F32) for rank in ranks).astype(BF)
+        out[NEW_TOK:after] = up_ref[request]
+    rows = pl.ds(pl.multiple_of(half * NEW_TOK, NEW_TOK), NEW_TOK)
+    for part in range(4):
+        start = after + part * NEW_TOK
+        cols = slice(part * WIDTH, (part + 1) * WIDTH)
+        outs[0][start : start + NEW_TOK] = (
+            base_ref[rows, cols].astype(F32) + got_ref[:, cols].astype(F32)
+        ).astype(BF)
+
+
+def parcels(where, base, got, ups, ranks):
     whole = pl.BlockSpec(memory_space=pltpu.VMEM)
-    return pl.pallas_call(
-        seq_kernel,
-        in_specs=[pl.BlockSpec(memory_space=pltpu.SMEM)] + [whole] * 4,
-        out_specs=[whole] * 3,
+    height = NEW_TOK + ups.shape[1]
+    return pl.pallas_call(
+        parcel_kernel,
+        in_specs=[pl.BlockSpec(memory_space=pltpu.SMEM)] + [whole] * 7,
+        out_specs=[whole, whole],
         out_shape=[
-            jax.ShapeDtypeStruct((NEW_TOK, WIDTH), BF),
-            jax.ShapeDtypeStruct((NEW_TOK, 4 * WIDTH), F32),
-            jax.ShapeDtypeStruct((4, parts[0].shape[0] - 5 * NEW_TOK, WIDTH), BF),
+            jax.ShapeDtypeStruct((height + 4 * NEW_TOK, WIDTH), BF),
+            jax.ShapeDtypeStruct((height, WIDTH), BF),
         ],
         compiler_params=pltpu.CompilerParams(vmem_limit_bytes=SMALL_VMEM),
-        name="seq_sum",
-    )(where, *parts)
+        name="tensor_sum",
+    )(where, base, got, ups, *ranks)
 
 
 def merge_kernel(*refs):
@@ -420,11 +419,21 @@
     )(*parts)
 
 
-def final_kernel(where, q_ref, cos_ref, sin_ref, up_ref, mean_ref, log_ref, base_ref, *rest):
-    ranks, (kv_out, attention_out, wide) = rest[:4], rest[4:]
+def final_kernel(where, q_ref, cos_ref, sin_ref, mean_ref, log_ref, *rest):
+    parts, (kv_out, attention_out, wide, up_ref) = rest[:4], rest[4:]
     half = q_ref.shape[0]
     start = pl.multiple_of(where[PARITY] * half, half)
-    rank = sum(r[...].astype(F32) for r in ranks).astype(BF)
+    after = NEW_TOK + up_ref.shape[1]
+    rank = sum(part[:NEW_TOK].astype(F32) for part in parts).astype(BF)
+    for step, part in enumerate(parts):
+        up_ref[jnp.bitwise_xor(where[SEQ], step)] = part[NEW_TOK:after]
+    base = [
+        sum(
+            part[after + col * NEW_TOK : after + (col + 1) * NEW_TOK].astype(F32)
+            for part in parts[:2]
+        )
+        for col in range(4)
+    ]
     keys, values = [], []
     for h in range(2):
         for e in range(2):
@@ -432,7 +441,7 @@
                 rank[:, e * 64 : (e + 1) * 64], up_ref[2 * e + h], preferred_element_type=F32
             )
             part = 2 * h + e
-            field = base_ref[:, part * WIDTH : (part + 1) * WIDTH] + delta
+            field = base[part] + delta
             if e == 0:
                 field = field * cos_ref[...] + pltpu.roll(field, WIDTH // 2, 1) * sin_ref[...]
             wide[pl.ds(part, NEW_TOK, stride=4), :] = field
@@ -463,13 +472,13 @@
             attention_out[:, n * WIDTH : (n + 1) * WIDTH] = out[j * half : (j + 1) * half]
 
 
-def final(where, queries, cos, sin, up, mean, log, base, ranks):
+def final(where, queries, cos, sin, mean, log, parts):
     half, width = NEW_TOK // 2, queries.shape[1]
 
     def whole(a):
         return pl.BlockSpec(a.shape, lambda i, w: (0,) * a.ndim)
 
-    rest = [cos, sin, up, mean, log, base, *ranks]
+    rest = [cos, sin, mean, log, *parts]
     return pl.pallas_call(
         final_kernel,
         grid_spec=pltpu.PrefetchScalarGridSpec(
@@ -481,7 +490,10 @@
                 pl.BlockSpec((half * 4, WIDTH), lambda i, w: (0, 0)),
                 pl.BlockSpec((half, width), lambda i, w: (0, 0)),
             ],
-            scratch_shapes=[pltpu.VMEM((NEW_TOK * 4, WIDTH), F32)],
+            scratch_shapes=[
+                pltpu.VMEM((NEW_TOK * 4, WIDTH), F32),
+                pltpu.VMEM((4, parts[0].shape[0] - 5 * NEW_TOK, WIDTH), BF),
+            ],
         ),
         out_shape=[
             jax.ShapeDtypeStruct((half * 4, WIDTH), BF),
@@ -553,18 +565,19 @@
     received = lax.optimization_barrier((*received, *sent))[:3]
     base = (parts[0].astype(F32) + sum(r.astype(F32) for r in received)).astype(BF)
     got2 = flip("seq", 2)(tie(o2, *sent))
-    o0, o1 = attend(tie(where, *sent, base), queries, cache_rows, False)
+    base_other = lax.dynamic_slice_in_dim(base, (1 - seq // 2) * NEW_TOK, NEW_TOK, 0)
+    o0, o1 = attend(tie(where, *sent, base, base_other), queries, cache_rows, False)
+    got_base = flip("seq", 3)(tie(base_other, o1))
 
     cos, sin = rotary_tables()
-    mine, others = rank_parts(tie(where, o1, cos, sin, got2), hidden, base, maps, came)
-    rank, base, ups = seq_sum(
-        where, [mine, flip("seq", 1)(mine), flip("seq", 2)(others), flip("seq", 3)(others)]
-    )
+    rank, ups = rank_parts(tie(where, o1, cos, sin, got2), hidden, maps, came)
     got1, got3 = flip("seq", 1)(tie(o1, rank)), flip("seq", 3)(tie(o3, rank))
     ranks = [rank] + [shift("tensor", step)(rank) for step in (1, 2, 3)]
-    mean, log = merge(list(lax.optimization_barrier((o0, got1, got2, got3, rank)))[:4])
-
-    new_kv, attention = final(where, queries, cos, sin, ups, mean, log, base, ranks)
+    mine, others = parcels(where, base, got_base, ups, ranks)
+    parts = [mine, flip("seq", 1)(mine), flip("seq", 2)(others), flip("seq", 3)(others)]
+    mean, log = merge(list(lax.optimization_barrier((o0, got1, got2, got3, mine)))[:4])
+
+    new_kv, attention = final(where, queries, cos, sin, mean, log, parts)
     return new_kv.reshape(-1, 2, 2, WIDTH), attention
 
 

time: 87.1 us -> 84 us (0.964); the launches traced: 87.9 us -> 83 us
  waiting for transfers between devices: 17.8 us -> 9.11 us
  starting transfers between devices: 30.1 us -> 33.3 us
    ppermute x8 -> x9, waiting for transfers between devices: 12.7 us -> 3.29 us  [flip(): lax.ppermute(a, axis, [(i, i ^ mask) for i in range(lax.axis_size(axis))])]
    ppermute x8 -> x9, starting transfers between devices: 9.25 us -> 13.2 us  [flip(): lax.ppermute(a, axis, [(i, i ^ mask) for i in range(lax.axis_size(axis))])]
  transfers between devices with their start and end apart: 20 -> 21, of which waited for: 6 -> 7; matrix products, arithmetic and copies ran while one was open for 1% -> 2% of each run, Pallas kernels for 38% -> 42%
where the time goes in v1:
time: 84 us; the launch traced here: 83 us
  Pallas kernels  38.5 us (46%)
  starting transfers between devices  33.3 us (40%)
  waiting for transfers between devices  9.11 us (11%)
  between operations  0.84 us (1%)
    pallas_call x2, Pallas kernels, attend(): pl.pallas_call(attend_kernel, grid_spec=pltpu.PrefetchScalarGridSpec(num_...  25.2 us
    ppermute x12, starting transfers between devices, shift(): lax.ppermute(a, axis, [(i, (i + step) % size) for i in range(size)])  20 us
    ppermute x9, starting transfers between devices, flip(): lax.ppermute(a, axis, [(i, i ^ mask) for i in range(lax.axis_size(axis))])  13.2 us
    ppermute x12, waiting for transfers between devices, shift(): lax.ppermute(a, axis, [(i, (i + step) % size) for i in range(size)])  5.82 us
    pallas_call x1, Pallas kernels, prep(): pl.pallas_call(prep_kernel, in_specs=[pl.BlockSpec(memory_space=pltpu.SME...  4.99 us
    pallas_call x2, Pallas kernels, relay(): pl.pallas_call(functools.partial(relay_kernel, slots, len(came)), in_spec...  3.55 us
    ppermute x9, waiting for transfers between devices, flip(): lax.ppermute(a, axis, [(i, i ^ mask) for i in range(lax.axis_size(axis))])  3.29 us
    pallas_call x1, Pallas kernels, final(): pl.pallas_call(final_kernel, grid_spec=pltpu.PrefetchScalarGridSpec(num_s...  2.23 us
  transfers between devices with their start and end apart: 21, of which 7 were waited for; matrix products, arithmetic and copies ran while one was open for 2% of the time, Pallas kernels for 42%

profile of v1, /device:TPU:32, one launch (start us, length us, event | category | flops | bytes accessed | tf_op | source)
XLA Modules:
  0.0 83.0 jit_solution(13724547439003629897)
XLA Ops:
  0.6 0.1 collective-permute-start
  0.7 0.5 collective-permute-start.1
  1.3 0.7 concatenate.9.where
  2.0 0.3 fusion
  2.3 0.9 %collective-permute-done.1.refs_3_ = bf16[4,2,64,256]{3,2,1,0:T(8,128)(2,1)S(1)} collective-permute-done((bf16[4,2,64,256]{3,2,1,0:T(8,128)(2,1)}, bf16[4,2,64,256]{3,2,1,0:T(8,128)(2,1)S(1)}, u32[]{:S(2)}, u32[]{:S(2)}) %collective-permute-start.1) | collective-permute-done | bytes 262176 | tf_op jit(solution)/shard_map/ppermute | solution.py:517
  3.2 0.0 collective-permute-done.refs_2_
  3.2 1.6 %relay_far.1 = (bf16[3,576,128]{2,1,0:T(8,128)(2,1)S(1)}, bf16[3,576,128]{2,1,0:T(8,128)(2,1)S(1)}) custom-call(s32[38]{0:T(128)S(1)} %concatenate.9.where, bf16[4,512,128]{2,1,0:T(8,128)(2,1)} %refs_0_.5, bf16[4,2,64,256]{3,2,1,0:T(8,128)(2,1)} %refs_1_.5, bf16[4,512,128]{2,1,0:T(8,128)(2,1)S(1)} %collective-permute-done.refs_2_, ...), custom_call_target="tpu_custom_call" | custom-call | bytes 2097152 | tf_op jit(solution)/shard_map/relay_far/pallas_call | solution.py:283
  4.8 2.6 %collective-permute-start.2 = (bf16[3,576,128]{2,1,0:T(8,128)(2,1)S(1)}, bf16[3,576,128]{2,1,0:T(8,128)(2,1)S(1)}, u32[]{:S(2)}, u32[]{:S(2)}) collective-permute-start(bf16[3,576,128]{2,1,0:T(8,128)(2,1)S(1)} %get-tuple-element.42), channel_id=1, source_target_pairs={{0,64},{16,80},{32,96},{48,112},{64,128},{80,144},{96,160},{112,17... | collective-permute-start | bytes 1327112 | tf_op jit(solution)/shard_map/ppermute | solution.py:524
  7.4 2.2 %collective-permute-start.3 = (bf16[3,576,128]{2,1,0:T(8,128)(2,1)S(1)}, bf16[3,576,128]{2,1,0:T(8,128)(2,1)S(1)}, u32[]{:S(2)}, u32[]{:S(2)}) collective-permute-start(bf16[3,576,128]{2,1,0:T(8,128)(2,1)S(1)} %get-tuple-element.43), channel_id=1, source_target_pairs={{0,192},{16,208},{32,224},{48,240},{64,0},{80,16},{96,32},{112,48}... | collective-permute-start | bytes 1327112 | tf_op jit(solution)/shard_map/ppermute | solution.py:524
  9.7 5.0 %base_partial.1 = (bf16[256,512]{1,0:T(8,128)(2,1)S(1)}, bf16[256,512]{1,0:T(8,128)(2,1)S(1)}, bf16[256,512]{1,0:T(8,128)(2,1)S(1)}, bf16[256,512]{1,0:T(8,128)(...) custom-call(s32[38]{0:T(128)S(1)} %concatenate.9.where, bf16[256,512]{1,0:T(8,128)(2,1)} %hidden_ref.1, ...), custom_call_target="tpu_custom_call" | custom-call | flops 536870912 | bytes 11534336 | tf_op jit(solution)/shard_map/base_partial/pallas_call | solution.py:78
  14.7 1.6 %collective-permute-start.4 = (bf16[256,512]{1,0:T(8,128)(2,1)S(1)}, bf16[256,512]{1,0:T(8,128)(2,1)S(1)}, u32[]{:S(2)}, u32[]{:S(2)}) collective-permute-start(bf16[256,512]{1,0:T(8,128)(2,1)S(1)} %get-tuple-element.55), channel_id=1, source_target_pairs={{0,4},{4,8},{8,12},{12,0},{1,5},{5,9},{9,13},{13,1},{2,6},{6,10},{... | collective-permute-start | bytes 786440 | tf_op jit(solution)/shard_map/ppermute | solution.py:524
  16.2 2.7 %collective-permute-start.5 = (bf16[256,512]{1,0:T(8,128)(2,1)S(1)}, bf16[256,512]{1,0:T(8,128)(2,1)S(1)}, u32[]{:S(2)}, u32[]{:S(2)}) collective-permute-start(bf16[256,512]{1,0:T(8,128)(2,1)S(1)} %get-tuple-element.56), channel_id=1, source_target_pairs={{0,8},{4,12},{8,0},{12,4},{1,9},{5,13},{9,1},{13,5},{2,10},{6,14},... | collective-permute-start | bytes 786440 | tf_op jit(solution)/shard_map/ppermute | solution.py:524
  19.0 1.4 %collective-permute-start.6 = (bf16[256,512]{1,0:T(8,128)(2,1)S(1)}, bf16[256,512]{1,0:T(8,128)(2,1)S(1)}, u32[]{:S(2)}, u32[]{:S(2)}) collective-permute-start(bf16[256,512]{1,0:T(8,128)(2,1)S(1)} %get-tuple-element.57), channel_id=1, source_target_pairs={{0,12},{4,0},{8,4},{12,8},{1,13},{5,1},{9,5},{13,9},{2,14},{6,2},{... | collective-permute-start | bytes 786440 | tf_op jit(solution)/shard_map/ppermute | solution.py:524
  20.4 12.6 %attend_other.1 = (bf16[64,2176]{1,0:T(8,128)(2,1)S(1)}, bf16[64,2176]{1,0:T(8,128)(2,1)S(1)}) custom-call(s32[38]{0:T(128)S(1)} %concatenate.9.where, bf16[256,2048]{1,0:T(8,128)(2,1)S(1)} %get-tuple-element.45.q_ref, bf16[32768,128]{1,0:T(8,128)(2,1)S(1)} %get-tuple-element.48.x_ref), custom_call_target="tpu_custom_call" | custom-call | flops 8589934592 | bytes 5242880 | tf_op jit(solution)/shard_map/attend_other/pallas_call | solution.py:190
  33.0 0.0 collective-permute-done.2.refs_4_
  33.0 0.0 collective-permute-done.3.refs_5_
  33.0 1.9 %relay_near.1 = (bf16[2,576,128]{2,1,0:T(8,128)(2,1)S(1)}, bf16[2,576,128]{2,1,0:T(8,128)(2,1)S(1)}, bf16[2,576,128]{2,1,0:T(8,128)(2,1)S(1)}, bf16[2,576,128]{2,1,0:T(8,128)(2,1)S(1)}) custom-call(s32[38]{0:T(128)S(1)} %concatenate.9.where, bf16[4,512,128]{2,1,0:T(8,128)(2,1)} %refs_0_.5, bf16[4,2,64,256]{3,2,1,0:T(8,128)(2,1)} %refs_1_.5, ...), custom_call_target="tpu_custom_call" | custom-call | bytes 2097152 | tf_op jit(solution)/shard_map/relay_near/pallas_call | solution.py:283
  34.9 1.2 %collective-permute-start.10 = (bf16[2,576,128]{2,1,0:T(8,128)(2,1)S(1)}, bf16[2,576,128]{2,1,0:T(8,128)(2,1)S(1)}, u32[]{:S(2)}, u32[]{:S(2)}) collective-permute-start(bf16[2,576,128]{2,1,0:T(8,128)(2,1)S(1)} %get-tuple-element.53), channel_id=1, source_target_pairs={{0,224},{16,240},{32,0},{48,16},{64,32},{80,48},{96,64},{112,80},{... | collective-permute-start | bytes 884744 | tf_op jit(solution)/shard_map/ppermute | solution.py:524
  36.2 3.6 %collective-permute-start.11 = (bf16[2,576,128]{2,1,0:T(8,128)(2,1)S(1)}, bf16[2,576,128]{2,1,0:T(8,128)(2,1)S(1)}, u32[]{:S(2)}, u32[]{:S(2)}) collective-permute-start(bf16[2,576,128]{2,1,0:T(8,128)(2,1)S(1)} %get-tuple-element.54), channel_id=1, source_target_pairs={{0,192},{16,208},{32,224},{48,240},{64,0},{80,16},{96,32},{112,48}... | collective-permute-start | bytes 884744 | tf_op jit(solution)/shard_map/ppermute | solution.py:524
  39.8 0.0 collective-permute-done.4
  39.8 0.0 collective-permute-start.8
  39.8 0.0 collective-permute-done.5
  39.8 1.4 %collective-permute-start.9 = (bf16[2,576,128]{2,1,0:T(8,128)(2,1)S(1)}, bf16[2,576,128]{2,1,0:T(8,128)(2,1)S(1)}, u32[]{:S(2)}, u32[]{:S(2)}) collective-permute-start(bf16[2,576,128]{2,1,0:T(8,128)(2,1)S(1)} %get-tuple-element.52), channel_id=1, source_target_pairs={{0,64},{16,80},{32,96},{48,112},{64,128},{80,144},{96,160},{112,17... | collective-permute-start | bytes 884744 | tf_op jit(solution)/shard_map/ppermute | solution.py:524
  41.2 0.0 collective-permute-done.6
  41.2 0.1 add_convert_fusion.base_ref
  41.4 0.0 copy-start
  41.4 3.5 %collective-permute-start.7 = (bf16[64,2176]{1,0:T(8,128)(2,1)S(1)}, bf16[64,2176]{1,0:T(8,128)(2,1)S(1)}, u32[]{:S(2)}, u32[]{:S(2)}) collective-permute-start(bf16[64,2176]{1,0:T(8,128)(2,1)S(1)} %get-tuple-element.64), channel_id=1, source_target_pairs={{0,2},{1,3},{2,0},{3,1},{4,6},{5,7},{6,4},{7,5},{8,10},{9,11},{10,... | collective-permute-start | bytes 835592 | tf_op jit(solution)/shard_map/ppermute | solution.py:517
  44.9 12.6 %attend_own.1 = (bf16[64,2176]{1,0:T(8,128)(2,1)S(1)}, bf16[64,2176]{1,0:T(8,128)(2,1)S(1)}) custom-call(s32[38]{0:T(128)S(1)} %concatenate.9.where, bf16[256,2048]{1,0:T(8,128)(2,1)S(1)} %get-tuple-element.45.q_ref, bf16[32768,128]{1,0:T(8,128)(2,1)S(1)} %get-tuple-element.48.x_ref), custom_call_target="tpu_custom_call" | custom-call | flops 8589934592 | bytes 5242880 | tf_op jit(solution)/shard_map/attend_own/pallas_call | solution.py:190
  57.5 0.0 collective-permute-done.7.refs_2_
  57.5 1.1 %collective-permute-start.14 = (bf16[128,512]{1,0:T(8,128)(2,1)S(1)}, bf16[128,512]{1,0:T(8,128)(2,1)S(1)}, u32[]{:S(2)}, u32[]{:S(2)}) collective-permute-start(bf16[128,512]{1,0:T(8,128)(2,1)S(1)} %constant_dynamic-slice_fusion), channel_id=1, source_target_pairs={{0,3},{1,2},{2,1},{3,0},{4,7},{5,6},{6,5},{7,4},{8,11},{9,10},{10,... | collective-permute-start | bytes 393224 | tf_op jit(solution)/shard_map/ppermute | solution.py:517
  58.6 0.1 pad_maximum_fusion
  58.7 0.0 collective-permute-done.10.refs_6_
  58.7 0.0 collective-permute-done.11.refs_7_
  58.7 0.0 collective-permute-done.8.refs_4_
  58.8 2.0 %collective-permute-done.9.refs_5_ = bf16[2,576,128]{2,1,0:T(8,128)(2,1)S(1)} collective-permute-done((bf16[2,576,128]{2,1,0:T(8,128)(2,1)S(1)}, bf16[2,576,128]{2,1,0:T(8,128)(2,1)S(1)}, u32[]{:S(2)}, u32[]{:S(2)}) %collective-permute-start.9) | collective-permute-done | bytes 294944 | tf_op jit(solution)/shard_map/ppermute | solution.py:524
  60.8 0.0 copy-done
  60.8 1.1 %rank_partial.1 = (bf16[256,128]{1,0:T(8,128)(2,1)S(1)}, bf16[2,64,128]{2,1,0:T(8,128)(2,1)S(1)}) custom-call(s32[38]{0:T(128)S(1)} %concatenate.9.where, bf16[256,512]{1,0:T(8,128)(2,1)S(1)} %copy-done, bf16[4,512,128]{2,1,0:T(8,128)(2,1)} %refs_0_.5, bf16[4,2,64,256]{3,2,1,0:T(8,128)(2,1)} %refs_1_.5, ...), custom_call_target="tpu_custom_call" | custom-call | tf_op jit(solution)/shard_map/rank_partial/pallas_call | solution.py:339
  61.8 3.1 %collective-permute-start.13 = (bf16[64,2176]{1,0:T(8,128)(2,1)S(1)}, bf16[64,2176]{1,0:T(8,128)(2,1)S(1)}, u32[]{:S(2)}, u32[]{:S(2)}) collective-permute-start(bf16[64,2176]{1,0:T(8,128)(2,1)S(1)} %get-tuple-element.69), channel_id=1, source_target_pairs={{0,3},{1,2},{2,1},{3,0},{4,7},{5,6},{6,5},{7,4},{8,11},{9,10},{10,... | collective-permute-start | bytes 835592 | tf_op jit(solution)/shard_map/ppermute | solution.py:517
  64.9 0.1 collective-permute-start.12
  65.1 0.5 collective-permute-start.15
  65.6 1.2 %collective-permute-start.16 = (bf16[256,128]{1,0:T(8,128)(2,1)S(1)}, bf16[256,128]{1,0:T(8,128)(2,1)S(1)}, u32[]{:S(2)}, u32[]{:S(2)}) collective-permute-start(bf16[256,128]{1,0:T(8,128)(2,1)S(1)} %get-tuple-element.66.refs_0_), channel_id=1, source_target_pairs={{0,8},{4,12},{8,0},{12,4},{1,9},{5,13},{9,1},{13,5},{2,10},{6,14},... | collective-permute-start | bytes 196616 | tf_op jit(solution)/shard_map/ppermute | solution.py:524
  66.8 0.0 collective-permute-done.14.got_ref
  66.8 1.5 %collective-permute-start.17 = (bf16[256,128]{1,0:T(8,128)(2,1)S(1)}, bf16[256,128]{1,0:T(8,128)(2,1)S(1)}, u32[]{:S(2)}, u32[]{:S(2)}) collective-permute-start(bf16[256,128]{1,0:T(8,128)(2,1)S(1)} %get-tuple-element.66.refs_0_), channel_id=1, source_target_pairs={{0,12},{4,0},{8,4},{12,8},{1,13},{5,1},{9,5},{13,9},{2,14},{6,2},{... | collective-permute-start | bytes 196616 | tf_op jit(solution)/shard_map/ppermute | solution.py:524
  68.3 2.2 %collective-permute-done.15.refs_1_ = bf16[256,128]{1,0:T(8,128)(2,1)S(1)} collective-permute-done((bf16[256,128]{1,0:T(8,128)(2,1)S(1)}, bf16[256,128]{1,0:T(8,128)(2,1)S(1)}, u32[]{:S(2)}, u32[]{:S(2)}) %collective-permute-start.15) | collective-permute-done | bytes 65568 | tf_op jit(solution)/shard_map/ppermute | solution.py:524
  70.5 0.8 collective-permute-done.16.refs_2_
  71.4 0.7 collective-permute-done.17.refs_3_
  72.1 0.6 tensor_sum.1
  72.7 2.0 %collective-permute-start.18 = (bf16[704,128]{1,0:T(8,128)(2,1)S(1)}, bf16[704,128]{1,0:T(8,128)(2,1)S(1)}, u32[]{:S(2)}, u32[]{:S(2)}) collective-permute-start(bf16[704,128]{1,0:T(8,128)(2,1)S(1)} %get-tuple-element.72.rest_0_), channel_id=1, source_target_pairs={{0,1},{1,0},{2,3},{3,2},{4,5},{5,4},{6,7},{7,6},{8,9},{9,8},{10,11... | collective-permute-start | bytes 540680 | tf_op jit(solution)/shard_map/ppermute | solution.py:517
  74.7 0.6 collective-permute-start.19
  75.3 2.2 %collective-permute-start.20 = (bf16[192,128]{1,0:T(8,128)(2,1)S(1)}, bf16[192,128]{1,0:T(8,128)(2,1)S(1)}, u32[]{:S(2)}, u32[]{:S(2)}) collective-permute-start(bf16[192,128]{1,0:T(8,128)(2,1)S(1)} %get-tuple-element.79), channel_id=1, source_target_pairs={{0,3},{1,2},{2,1},{3,0},{4,7},{5,6},{6,5},{7,4},{8,11},{9,10},{10,... | collective-permute-start | bytes 147464 | tf_op jit(solution)/shard_map/ppermute | solution.py:517
  77.5 0.0 collective-permute-done.13.refs_3_
  77.5 0.0 collective-permute-done.12.refs_1_
  77.5 0.9 %merge_prefix.1 = (f32[1024,128]{1,0:T(8,128)S(1)}, f32[1024,128]{1,0:T(8,128)S(1)}) custom-call(bf16[64,2176]{1,0:T(8,128)(2,1)S(1)} %get-tuple-element.73.refs_0_, bf16[64,2176]{1,0:T(8,128)(2,1)S(1)} %collective-permute-done.12.refs_1_, bf16[64,2176]{1,0:T(8,128)(2,1)S(1)} %collective-permute-done.7.refs_2_, ...), custom_call_target="tpu_custom_call" | custom-call | tf_op jit(solution)/shard_map/merge_prefix/pallas_call | solution.py:412
  78.4 1.9 %collective-permute-done.19.rest_2_ = bf16[192,128]{1,0:T(8,128)(2,1)S(1)} collective-permute-done((bf16[192,128]{1,0:T(8,128)(2,1)S(1)}, bf16[192,128]{1,0:T(8,128)(2,1)S(1)}, u32[]{:S(2)}, u32[]{:S(2)}) %collective-permute-start.19) | collective-permute-done | bytes 49184 | tf_op jit(solution)/shard_map/ppermute | solution.py:517
  80.3 0.5 collective-permute-done.20.rest_3_
  80.8 0.0 collective-permute-done.18.rest_1_
  80.8 2.2 %new_kv_and_attention.1 = (bf16[256,128]{1,0:T(8,128)(2,1)}, bf16[64,2048]{1,0:T(8,128)(2,1)}) custom-call(s32[38]{0:T(128)S(1)} %concatenate.9.where, bf16[256,2048]{1,0:T(8,128)(2,1)S(1)} %get-tuple-element.45.q_ref, f32[128,128]{1,0:T(8,128)S(1)} %get-tuple-element.85.cos_ref, f32[128,128]{1,0:T(8,128)S(1)} %get-tuple-element.86.sin_ref, ...), custom_call_target="tpu_custom_call" | custom-call | tf_op jit(solution)/shard_map/new_kv_and_attention/pallas_call | solution.py:482
  (3 shorter events, 0.0 us)
Async XLA Ops:
  0.6 2.6 %collective-permute-start = (bf16[4,512,128]{2,1,0:T(8,128)(2,1)}, bf16[4,512,128]{2,1,0:T(8,128)(2,1)S(1)}, u32[]{:S(2)}, u32[]{:S(2)}) collective-permute-start(bf16[4,512,128]{2,1,0:T(8,128)(2,1)} %refs_0_.5), channel_id=1, source_target_pairs={{0,16},{16,0},{32,48},{48,32},{64,80},{80,64},{96,112},{112,96},{1... | collective-permute-start | bytes 1572872 | tf_op jit(solution)/shard_map/ppermute | solution.py:517
  0.7 2.5 %collective-permute-start.1 = (bf16[4,2,64,256]{3,2,1,0:T(8,128)(2,1)}, bf16[4,2,64,256]{3,2,1,0:T(8,128)(2,1)S(1)}, u32[]{:S(2)}, u32[]{:S(2)}) collective-permute-start(bf16[4,2,64,256]{3,2,1,0:T(8,128)(2,1)} %refs_1_.5), channel_id=1, source_target_pairs={{0,16},{16,0},{32,48},{48,32},{64,80},{80,64},{96,112},{112,96},{1... | collective-permute-start | bytes 786440 | tf_op jit(solution)/shard_map/ppermute | solution.py:517
  4.8 28.1 %collective-permute-start.2 = (bf16[3,576,128]{2,1,0:T(8,128)(2,1)S(1)}, bf16[3,576,128]{2,1,0:T(8,128)(2,1)S(1)}, u32[]{:S(2)}, u32[]{:S(2)}) collective-permute-start(bf16[3,576,128]{2,1,0:T(8,128)(2,1)S(1)} %get-tuple-element.42), channel_id=1, source_target_pairs={{0,64},{16,80},{32,96},{48,112},{64,128},{80,144},{96,160},{112,17... | collective-permute-start | bytes 1327112 | tf_op jit(solution)/shard_map/ppermute | solution.py:524
  7.4 25.6 %collective-permute-start.3 = (bf16[3,576,128]{2,1,0:T(8,128)(2,1)S(1)}, bf16[3,576,128]{2,1,0:T(8,128)(2,1)S(1)}, u32[]{:S(2)}, u32[]{:S(2)}) collective-permute-start(bf16[3,576,128]{2,1,0:T(8,128)(2,1)S(1)} %get-tuple-element.43), channel_id=1, source_target_pairs={{0,192},{16,208},{32,224},{48,240},{64,0},{80,16},{96,32},{112,48}... | collective-permute-start | bytes 1327112 | tf_op jit(solution)/shard_map/ppermute | solution.py:524
  14.7 25.1 %collective-permute-start.4 = (bf16[256,512]{1,0:T(8,128)(2,1)S(1)}, bf16[256,512]{1,0:T(8,128)(2,1)S(1)}, u32[]{:S(2)}, u32[]{:S(2)}) collective-permute-start(bf16[256,512]{1,0:T(8,128)(2,1)S(1)} %get-tuple-element.55), channel_id=1, source_target_pairs={{0,4},{4,8},{8,12},{12,0},{1,5},{5,9},{9,13},{13,1},{2,6},{6,10},{... | collective-permute-start | bytes 786440 | tf_op jit(solution)/shard_map/ppermute | solution.py:524
  16.2 23.6 %collective-permute-start.5 = (bf16[256,512]{1,0:T(8,128)(2,1)S(1)}, bf16[256,512]{1,0:T(8,128)(2,1)S(1)}, u32[]{:S(2)}, u32[]{:S(2)}) collective-permute-start(bf16[256,512]{1,0:T(8,128)(2,1)S(1)} %get-tuple-element.56), channel_id=1, source_target_pairs={{0,8},{4,12},{8,0},{12,4},{1,9},{5,13},{9,1},{13,5},{2,10},{6,14},... | collective-permute-start | bytes 786440 | tf_op jit(solution)/shard_map/ppermute | solution.py:524
  19.0 22.2 %collective-permute-start.6 = (bf16[256,512]{1,0:T(8,128)(2,1)S(1)}, bf16[256,512]{1,0:T(8,128)(2,1)S(1)}, u32[]{:S(2)}, u32[]{:S(2)}) collective-permute-start(bf16[256,512]{1,0:T(8,128)(2,1)S(1)} %get-tuple-element.57), channel_id=1, source_target_pairs={{0,12},{4,0},{8,4},{12,8},{1,13},{5,1},{9,5},{13,9},{2,14},{6,2},{... | collective-permute-start | bytes 786440 | tf_op jit(solution)/shard_map/ppermute | solution.py:524
  34.9 23.8 %collective-permute-start.10 = (bf16[2,576,128]{2,1,0:T(8,128)(2,1)S(1)}, bf16[2,576,128]{2,1,0:T(8,128)(2,1)S(1)}, u32[]{:S(2)}, u32[]{:S(2)}) collective-permute-start(bf16[2,576,128]{2,1,0:T(8,128)(2,1)S(1)} %get-tuple-element.53), channel_id=1, source_target_pairs={{0,224},{16,240},{32,0},{48,16},{64,32},{80,48},{96,64},{112,80},{... | collective-permute-start | bytes 884744 | tf_op jit(solution)/shard_map/ppermute | solution.py:524
  36.2 22.6 %collective-permute-start.11 = (bf16[2,576,128]{2,1,0:T(8,128)(2,1)S(1)}, bf16[2,576,128]{2,1,0:T(8,128)(2,1)S(1)}, u32[]{:S(2)}, u32[]{:S(2)}) collective-permute-start(bf16[2,576,128]{2,1,0:T(8,128)(2,1)S(1)} %get-tuple-element.54), channel_id=1, source_target_pairs={{0,192},{16,208},{32,224},{48,240},{64,0},{80,16},{96,32},{112,48}... | collective-permute-start | bytes 884744 | tf_op jit(solution)/shard_map/ppermute | solution.py:524
  39.8 19.0 %collective-permute-start.8 = (bf16[2,576,128]{2,1,0:T(8,128)(2,1)S(1)}, bf16[2,576,128]{2,1,0:T(8,128)(2,1)S(1)}, u32[]{:S(2)}, u32[]{:S(2)}) collective-permute-start(bf16[2,576,128]{2,1,0:T(8,128)(2,1)S(1)} %get-tuple-element.51), channel_id=1, source_target_pairs={{0,32},{16,48},{32,64},{48,80},{64,96},{80,112},{96,128},{112,144}... | collective-permute-start | bytes 884744 | tf_op jit(solution)/shard_map/ppermute | solution.py:524
  39.8 21.0 %collective-permute-start.9 = (bf16[2,576,128]{2,1,0:T(8,128)(2,1)S(1)}, bf16[2,576,128]{2,1,0:T(8,128)(2,1)S(1)}, u32[]{:S(2)}, u32[]{:S(2)}) collective-permute-start(bf16[2,576,128]{2,1,0:T(8,128)(2,1)S(1)} %get-tuple-element.52), channel_id=1, source_target_pairs={{0,64},{16,80},{32,96},{48,112},{64,128},{80,144},{96,160},{112,17... | collective-permute-start | bytes 884744 | tf_op jit(solution)/shard_map/ppermute | solution.py:524
  41.4 19.4 %copy-start = (bf16[256,512]{1,0:T(8,128)(2,1)S(1)}, bf16[256,512]{1,0:T(8,128)(2,1)}, u32[]{:S(2)}) copy-start(bf16[256,512]{1,0:T(8,128)(2,1)} %hidden_ref.1) | copy-start | bytes 786436
  41.4 16.1 %collective-permute-start.7 = (bf16[64,2176]{1,0:T(8,128)(2,1)S(1)}, bf16[64,2176]{1,0:T(8,128)(2,1)S(1)}, u32[]{:S(2)}, u32[]{:S(2)}) collective-permute-start(bf16[64,2176]{1,0:T(8,128)(2,1)S(1)} %get-tuple-element.64), channel_id=1, source_target_pairs={{0,2},{1,3},{2,0},{3,1},{4,6},{5,7},{6,4},{7,5},{8,10},{9,11},{10,... | collective-permute-start | bytes 835592 | tf_op jit(solution)/shard_map/ppermute | solution.py:517
  57.5 9.3 %collective-permute-start.14 = (bf16[128,512]{1,0:T(8,128)(2,1)S(1)}, bf16[128,512]{1,0:T(8,128)(2,1)S(1)}, u32[]{:S(2)}, u32[]{:S(2)}) collective-permute-start(bf16[128,512]{1,0:T(8,128)(2,1)S(1)} %constant_dynamic-slice_fusion), channel_id=1, source_target_pairs={{0,3},{1,2},{2,1},{3,0},{4,7},{5,6},{6,5},{7,4},{8,11},{9,10},{10,... | collective-permute-start | bytes 393224 | tf_op jit(solution)/shard_map/ppermute | solution.py:517
  61.8 15.7 %collective-permute-start.13 = (bf16[64,2176]{1,0:T(8,128)(2,1)S(1)}, bf16[64,2176]{1,0:T(8,128)(2,1)S(1)}, u32[]{:S(2)}, u32[]{:S(2)}) collective-permute-start(bf16[64,2176]{1,0:T(8,128)(2,1)S(1)} %get-tuple-element.69), channel_id=1, source_target_pairs={{0,3},{1,2},{2,1},{3,0},{4,7},{5,6},{6,5},{7,4},{8,11},{9,10},{10,... | collective-permute-start | bytes 835592 | tf_op jit(solution)/shard_map/ppermute | solution.py:517
  64.9 12.6 %collective-permute-start.12 = (bf16[64,2176]{1,0:T(8,128)(2,1)S(1)}, bf16[64,2176]{1,0:T(8,128)(2,1)S(1)}, u32[]{:S(2)}, u32[]{:S(2)}) collective-permute-start(bf16[64,2176]{1,0:T(8,128)(2,1)S(1)} %get-tuple-element.67), channel_id=1, source_target_pairs={{0,1},{1,0},{2,3},{3,2},{4,5},{5,4},{6,7},{7,6},{8,9},{9,8},{10,11... | collective-permute-start | bytes 835592 | tf_op jit(solution)/shard_map/ppermute | solution.py:517
  65.1 5.5 %collective-permute-start.15 = (bf16[256,128]{1,0:T(8,128)(2,1)S(1)}, bf16[256,128]{1,0:T(8,128)(2,1)S(1)}, u32[]{:S(2)}, u32[]{:S(2)}) collective-permute-start(bf16[256,128]{1,0:T(8,128)(2,1)S(1)} %get-tuple-element.66.refs_0_), channel_id=1, source_target_pairs={{0,4},{4,8},{8,12},{12,0},{1,5},{5,9},{9,13},{13,1},{2,6},{6,10},{... | collective-permute-start | bytes 196616 | tf_op jit(solution)/shard_map/ppermute | solution.py:524
  65.6 5.8 %collective-permute-start.16 = (bf16[256,128]{1,0:T(8,128)(2,1)S(1)}, bf16[256,128]{1,0:T(8,128)(2,1)S(1)}, u32[]{:S(2)}, u32[]{:S(2)}) collective-permute-start(bf16[256,128]{1,0:T(8,128)(2,1)S(1)} %get-tuple-element.66.refs_0_), channel_id=1, source_target_pairs={{0,8},{4,12},{8,0},{12,4},{1,9},{5,13},{9,1},{13,5},{2,10},{6,14},... | collective-permute-start | bytes 196616 | tf_op jit(solution)/shard_map/ppermute | solution.py:524
  66.8 5.3 %collective-permute-start.17 = (bf16[256,128]{1,0:T(8,128)(2,1)S(1)}, bf16[256,128]{1,0:T(8,128)(2,1)S(1)}, u32[]{:S(2)}, u32[]{:S(2)}) collective-permute-start(bf16[256,128]{1,0:T(8,128)(2,1)S(1)} %get-tuple-element.66.refs_0_), channel_id=1, source_target_pairs={{0,12},{4,0},{8,4},{12,8},{1,13},{5,1},{9,5},{13,9},{2,14},{6,2},{... | collective-permute-start | bytes 196616 | tf_op jit(solution)/shard_map/ppermute | solution.py:524
  72.7 8.1 %collective-permute-start.18 = (bf16[704,128]{1,0:T(8,128)(2,1)S(1)}, bf16[704,128]{1,0:T(8,128)(2,1)S(1)}, u32[]{:S(2)}, u32[]{:S(2)}) collective-permute-start(bf16[704,128]{1,0:T(8,128)(2,1)S(1)} %get-tuple-element.72.rest_0_), channel_id=1, source_target_pairs={{0,1},{1,0},{2,3},{3,2},{4,5},{5,4},{6,7},{7,6},{8,9},{9,8},{10,11... | collective-permute-start | bytes 540680 | tf_op jit(solution)/shard_map/ppermute | solution.py:517
  74.7 5.6 %collective-permute-start.19 = (bf16[192,128]{1,0:T(8,128)(2,1)S(1)}, bf16[192,128]{1,0:T(8,128)(2,1)S(1)}, u32[]{:S(2)}, u32[]{:S(2)}) collective-permute-start(bf16[192,128]{1,0:T(8,128)(2,1)S(1)} %get-tuple-element.79), channel_id=1, source_target_pairs={{0,2},{1,3},{2,0},{3,1},{4,6},{5,7},{6,4},{7,5},{8,10},{9,11},{10,... | collective-permute-start | bytes 147464 | tf_op jit(solution)/shard_map/ppermute | solution.py:517
  75.3 5.5 %collective-permute-start.20 = (bf16[192,128]{1,0:T(8,128)(2,1)S(1)}, bf16[192,128]{1,0:T(8,128)(2,1)S(1)}, u32[]{:S(2)}, u32[]{:S(2)}) collective-permute-start(bf16[192,128]{1,0:T(8,128)(2,1)S(1)} %get-tuple-element.79), channel_id=1, source_target_pairs={{0,3},{1,2},{2,1},{3,0},{4,7},{5,6},{6,5},{7,4},{8,11},{9,10},{10,... | collective-permute-start | bytes 147464 | tf_op jit(solution)/shard_map/ppermute | solution.py:517
